TPU v7x, 512 devices: a whole 4x4x16 slice. The times are simulated.
512 devices in a mesh: seq: 32 (over z, core), blk: 16 (over x, y).
Axes of the slice: x: 4, y: 4, z: 16, core: 2. Of those that a mesh axis runs over, the one named last changes fastest.
Arguments:
- query: bfloat16 [65536, 4096], P(('seq', 'blk')), may hold values from -12 to 12
- key: bfloat16 [65536, 4096], P(('seq', 'blk')), may hold values from -80 to 80
- value: bfloat16 [65536, 4096], P(('seq', 'blk')), may hold values from -6 to 6
- recompute_index: int32 [3072], P(('seq', 'blk')), may hold values from 0 to 127, as said below
- counts: int32 [512], P(('seq', 'blk')), may hold values from 1 to 6, as said below
- timestep: int32 [1], replicated, may hold values from 0 to 49
- gate_table: float32 [50, 4096], replicated, may hold values from 0.5 to 2
Outputs:
- gated: bfloat16 [3072, 4096], P(('seq', 'blk'))
Inputs may be any that keep to these rules, and one draw needn't show every extreme that they name: `recompute_index`: the 6 positions of one device are distinct. `counts`: some device has all 6 slots live.
All inputs are finite; a program needn't handle non-finite values.
Results may differ from a plain program's by a relative error of at most 0.012.
Values may be sent and summed in bfloat16 or wider, within the bound.
No kernel may reach another device: no remote copies, remote signals or barrier semaphores. Data moves between devices by JAX's collectives and lax.ppermute only.
A program may use at most 64 MiB of HBM per device.

v0:
```python
import math

import jax
import jax.numpy as jnp
from jax import lax
from jax.sharding import PartitionSpec as P

HD = 128
HEADS = 32


def row_block(total):
    size = min(total, 512)
    while total % size != 0:
        size = size - 1
    return size


def partial_attention(queries, keys, values):
    total_rows, heads, depth = queries.shape
    size = row_block(total_rows)
    scale = 1.0 / math.sqrt(depth)

    def one_block(block):
        scores = jnp.einsum("rhd,khd->hrk", block, keys, preferred_element_type=jnp.float32) * scale
        top = jnp.max(scores, axis=2)
        powers = jnp.exp(scores - top[..., None])
        total = jnp.sum(powers, axis=2)
        mixed = jnp.einsum(
            "hrk,khd->rhd", powers.astype(jnp.bfloat16), values, preferred_element_type=jnp.float32
        )
        mixed = (mixed / total.T[..., None]).astype(jnp.bfloat16)
        return (mixed, top.T, total.T)

    blocks = queries.reshape(total_rows // size, size, heads, depth)
    mixed, top, total = lax.map(one_block, blocks)
    return (
        mixed.reshape(total_rows, heads, depth),
        top.reshape(total_rows, heads),
        total.reshape(total_rows, heads),
    )


def combine_parts(mixed, top, total):
    peak = jnp.max(top, axis=0)
    factor = total * jnp.exp(top - peak)
    summed = jnp.sum(factor[..., None] * mixed.astype(jnp.float32), axis=0)
    return (summed / jnp.sum(factor, axis=0)[..., None]).astype(jnp.bfloat16)


def local(query, key, value, recompute_index, counts, timestep, gate_table):
    seq_size = lax.axis_size("seq")
    blk_size = lax.axis_size("blk")
    slots = recompute_index.shape[0]
    width = query.shape[1]
    per_dev = HEADS // seq_size
    head_width = per_dev * HD
    chosen = query[recompute_index]
    keys, values = (
        lax.all_to_all(key, "seq", split_axis=1, concat_axis=0, tiled=True),
        lax.all_to_all(value, "seq", split_axis=1, concat_axis=0, tiled=True),
    )
    keys = keys.reshape(-1, per_dev, HD)
    values = values.reshape(-1, per_dev, HD)
    gathered = lax.all_gather(chosen, "blk", axis=0, tiled=True)
    spread = lax.all_to_all(gathered, "seq", split_axis=1, concat_axis=0, tiled=True)
    queries = spread.reshape(seq_size, blk_size, slots, head_width).transpose(1, 0, 2, 3)
    queries = queries.reshape(-1, per_dev, HD)
    mixed, top, total = partial_attention(queries, keys, values)
    mixed = mixed.reshape(blk_size, seq_size, slots, head_width)
    top = top.reshape(blk_size, seq_size, slots, per_dev)
    total = total.reshape(blk_size, seq_size, slots, per_dev)
    mixed = lax.all_to_all(
        lax.all_to_all(mixed, "seq", split_axis=1, concat_axis=3, tiled=True),
        "blk",
        split_axis=0,
        concat_axis=0,
        tiled=True,
    )
    top, total = (
        lax.all_to_all(
            lax.all_to_all(top, "seq", split_axis=1, concat_axis=3, tiled=True),
            "blk",
            split_axis=0,
            concat_axis=0,
            tiled=True,
        ),
        lax.all_to_all(
            lax.all_to_all(total, "seq", split_axis=1, concat_axis=3, tiled=True),
            "blk",
            split_axis=0,
            concat_axis=0,
            tiled=True,
        ),
    )
    attention = combine_parts(
        mixed.reshape(blk_size, slots, HEADS, HD),
        top.reshape(blk_size, slots, HEADS),
        total.reshape(blk_size, slots, HEADS),
    )
    attention = attention.reshape(slots, width)
    gate = lax.dynamic_index_in_dim(gate_table, timestep[0], 0, keepdims=False)
    gated = (gate[None, :] * attention.astype(jnp.float32)).astype(jnp.bfloat16)
    live = jnp.arange(slots, dtype=jnp.int32) < counts[0]
    return jnp.where(live[:, None], gated, jnp.zeros_like(gated))


def solution(mesh):
    in_specs = (
        P(("seq", "blk"), None),
        P(("seq", "blk"), None),
        P(("seq", "blk"), None),
        P(("seq", "blk")),
        P(("seq", "blk")),
        P(),
        P(),
    )
    out_specs = P(("seq", "blk"), None)
    return jax.shard_map(local, mesh=mesh, in_specs=in_specs, out_specs=out_specs, check_vma=False)
```

profile of v0, /device:TPU:1, one launch (start us, length us, event | category | flops | bytes accessed | tf_op | source)
XLA Modules:
  0.0 382.8 jit_solution(7330141485515167448)
XLA Ops:
  0.0 0.7 compare_select_fusion
  0.8 0.5 copy-done
  1.2 0.6 gather_fusion
  1.8 21.1 %all-gather.1 = bf16[16,6,4096]{2,1,0:T(8,128)(2,1)S(1)} all-gather(bf16[1,6,4096]{2,1,0:T(8,128)(2,1)S(1)} %bitcast.127), channel_id=2, replica_groups=mesh['seq'=32,'blk'=16] {'blk'}, dimensions={0}, use_global_device_ids=true | all-gather | bytes 835584 | tf_op jit(solution)/shard_map/all_gather | solution.py:65
  23.0 1.0 all_to_all.84
  23.9 1.2 copy.40
  25.1 20.8 %all-to-all-start = ((bf16[96,32,128]{2,0,1:T(8,128)(2,1)}), bf16[96,32,128]{2,0,1:T(8,128)(2,1)S(1)}, u32[]{:S(2)}, u32[]{:S(2)}) async-start(bf16[96,32,128]{2,0,1:T(8,128)(2,1)} %copy.40), calls=%async_computation | async-start | bytes 1572864 | tf_op jit(solution)/shard_map/all_to_all | solution.py:66
  45.9 2.3 copy.43
  48.2 42.4 %all-to-all-done = bf16[96,32,128]{2,0,1:T(8,128)(2,1)S(1)} async-done(((bf16[96,32,128]{2,0,1:T(8,128)(2,1)}), bf16[96,32,128]{2,0,1:T(8,128)(2,1)S(1)}, u32[]{:S(2)}, u32[]{:S(2)}) %all-to-all-start) | async-done | bytes 786464 | tf_op jit(solution)/shard_map/all_to_all | solution.py:66
  90.5 4.1 %all-to-all-start.1 = ((bf16[128,32,128]{0,2,1:T(8,128)(2,1)}), bf16[128,32,128]{0,2,1:T(8,128)(2,1)S(1)}, u32[]{:S(2)}, u32[]{:S(2)}) async-start(bf16[128,32,128]{0,2,1:T(8,128)(2,1)} %bitcast.17), calls=%async_computation.1 | async-start | bytes 2097152 | tf_op jit(solution)/shard_map/all_to_all | solution.py:60
  94.6 2.3 copy.45
  96.9 53.5 %all-to-all-done.1 = bf16[128,32,128]{0,2,1:T(8,128)(2,1)S(1)} async-done(((bf16[128,32,128]{0,2,1:T(8,128)(2,1)}), bf16[128,32,128]{0,2,1:T(8,128)(2,1)S(1)}, u32[]{:S(2)}, u32[]{:S(2)}) %all-to-all-start.1) | async-done | bytes 1048608 | tf_op jit(solution)/shard_map/all_to_all | solution.py:60
  150.4 5.3 %all-to-all-start.2 = ((bf16[128,32,128]{0,2,1:T(8,128)(2,1)}), bf16[128,32,128]{0,2,1:T(8,128)(2,1)}, u32[]{:S(2)}, u32[]{:S(2)}) async-start(bf16[128,32,128]{0,2,1:T(8,128)(2,1)} %bitcast.20), calls=%async_computation.2 | async-start | bytes 2097152 | tf_op jit(solution)/shard_map/all_to_all | solution.py:61
  156.4 1.2 reshape_reshape.12
  157.6 0.7 copy.44
  158.3 53.3 %all-to-all-done.2 = bf16[128,32,128]{0,2,1:T(8,128)(2,1)} async-done(((bf16[128,32,128]{0,2,1:T(8,128)(2,1)}), bf16[128,32,128]{0,2,1:T(8,128)(2,1)}, u32[]{:S(2)}, u32[]{:S(2)}) %all-to-all-start.2) | async-done | bytes 1048608 | tf_op jit(solution)/shard_map/all_to_all | solution.py:61
  211.6 1.6 copy.46
  213.2 35.4 %while.14 = (s32[]{:T(128)}, bf16[6,512,1,128]{3,1,2,0:T(8,128)(2,1)}, f32[6,512,1]{1,2,0:T(1,128)S(1)}, f32[6,512,1]{1,2,0:T(1,128)S(1)}, bf16[6,512,1,128]{3,1...) while((s32[]{:T(128)}, ...), condition=%wide.region_3.4_spmd, body=%wide.region_0.3_spmd.sunk | while | flops 1090649088 | bytes 27544664 | solution.py:36
  213.2 2.2 multiply_reduce_fusion.3
  215.5 1.5 fusion.38
  217.0 2.1 fusion.39
  219.1 2.2 multiply_reduce_fusion.3
  221.4 1.5 fusion.38
  222.9 2.1 fusion.39
  225.0 2.2 multiply_reduce_fusion.3
  227.3 1.5 fusion.38
  228.8 2.1 fusion.39
  230.9 2.2 multiply_reduce_fusion.3
  233.2 1.5 fusion.38
  234.7 2.1 fusion.39
  236.8 2.2 multiply_reduce_fusion.3
  239.0 1.5 fusion.38
  240.6 2.1 fusion.39
  242.7 2.2 multiply_reduce_fusion.3
  244.9 1.5 fusion.38
  246.5 2.1 fusion.39
  248.9 0.9 copy.52
  249.8 4.5 %all-to-all-start.5 = ((f32[16,32,6,1]{0,3,2,1:T(1,128)}), f32[16,32,6,1]{0,3,2,1:T(1,128)S(1)}, u32[]{:S(2)}, u32[]{:S(2)}) async-start(f32[16,32,6,1]{0,3,2,1:T(1,128)} %copy.52), calls=%async_computation.5 | async-start | bytes 196608 | tf_op jit(solution)/shard_map/all_to_all | solution.py:82
  254.6 0.9 copy.48
  255.5 13.1 %all-to-all-done.5 = f32[16,32,6,1]{0,3,2,1:T(1,128)S(1)} async-done(((f32[16,32,6,1]{0,3,2,1:T(1,128)}), f32[16,32,6,1]{0,3,2,1:T(1,128)S(1)}, u32[]{:S(2)}, u32[]{:S(2)}) %all-to-all-start.5) | async-done | bytes 12320 | tf_op jit(solution)/shard_map/all_to_all | solution.py:82
  268.6 5.3 %all-to-all-start.3 = ((f32[16,32,6,1]{0,3,2,1:T(1,128)}), f32[16,32,6,1]{0,3,2,1:T(1,128)S(1)}, u32[]{:S(2)}, u32[]{:S(2)}) async-start(f32[16,32,6,1]{0,3,2,1:T(1,128)} %copy.48), calls=%async_computation.3 | async-start | bytes 196608 | tf_op jit(solution)/shard_map/all_to_all | solution.py:89
  274.1 0.6 broadcast.57
  274.7 0.8 reduce.8
  275.4 0.7 reshape.106
  276.1 12.1 %all-to-all-done.3 = f32[16,32,6,1]{0,3,2,1:T(1,128)S(1)} async-done(((f32[16,32,6,1]{0,3,2,1:T(1,128)}), f32[16,32,6,1]{0,3,2,1:T(1,128)S(1)}, u32[]{:S(2)}, u32[]{:S(2)}) %all-to-all-start.3) | async-done | bytes 12320 | tf_op jit(solution)/shard_map/all_to_all | solution.py:89
  288.2 4.6 %all-to-all-start.6 = ((f32[16,1,192]{2,1,0:T(1,128)}), f32[16,1,192]{2,1,0:T(1,128)S(1)}, u32[]{:S(2)}, u32[]{:S(2)}) async-start(f32[16,1,192]{2,1,0:T(1,128)} %reshape.106), calls=%async_computation.6 | async-start | bytes 32768 | tf_op jit(solution)/shard_map/all_to_all | solution.py:81
  292.8 1.3 reshape_reshape.15
  294.1 1.8 copy.56
  295.9 3.3 all-to-all-done.6
  299.2 6.8 %all-to-all-start.7 = ((bf16[16,32,6,128]{3,0,2,1:T(8,128)(2,1)}), bf16[16,32,6,128]{3,0,2,1:T(8,128)(2,1)S(1)}, u32[]{:S(2)}, u32[]{:S(2)}) async-start(bf16[16,32,6,128]{3,0,2,1:T(8,128)(2,1)} %copy.56), calls=%async_computation.7 | async-start | bytes 1572864 | tf_op jit(solution)/shard_map/all_to_all | solution.py:74
  306.2 0.8 reduce.10
  307.0 0.7 reshape.108
  307.7 43.0 %all-to-all-done.7 = bf16[16,32,6,128]{3,0,2,1:T(8,128)(2,1)S(1)} async-done(((bf16[16,32,6,128]{3,0,2,1:T(8,128)(2,1)}), bf16[16,32,6,128]{3,0,2,1:T(8,128)(2,1)S(1)}, u32[]{:S(2)}, u32[]{:S(2)}) %all-to-all-start.7) | async-done | bytes 786464 | tf_op jit(solution)/shard_map/all_to_all | solution.py:74
  350.7 3.5 all-to-all-start.4
  355.1 1.8 reshape.103
  357.0 3.6 all-to-all-done.4
  360.6 4.3 %all-to-all-start.8 = ((bf16[16,1,6,4096]{3,2,1,0:T(8,128)(2,1)}), bf16[16,1,6,4096]{3,2,1,0:T(8,128)(2,1)}, u32[]{:S(2)}, u32[]{:S(2)}) async-start(bf16[16,1,6,4096]{3,2,1,0:T(8,128)(2,1)} %reshape.103), calls=%async_computation.8 | async-start | bytes 2097152 | tf_op jit(solution)/shard_map/all_to_all | solution.py:73
  364.9 0.9 constant_dynamic-slice_fusion
  366.5 0.7 reduce.9
  367.3 0.7 reduce.11
  368.6 1.4 mul.36
  370.2 9.5 %all-to-all-done.8 = bf16[16,1,6,4096]{3,2,1,0:T(8,128)(2,1)} async-done(((bf16[16,1,6,4096]{3,2,1,0:T(8,128)(2,1)}), bf16[16,1,6,4096]{3,2,1,0:T(8,128)(2,1)}, u32[]{:S(2)}, u32[]{:S(2)}) %all-to-all-start.8) | async-done | bytes 786464 | tf_op jit(solution)/shard_map/all_to_all | solution.py:73
  379.7 2.4 multiply_reduce_fusion.1
  382.1 0.7 fusion.27
  (29 shorter events, 2.7 us)
Async XLA Ops:
  0.0 1.2 copy-start
  25.1 65.4 %all-to-all-start = ((bf16[96,32,128]{2,0,1:T(8,128)(2,1)}), bf16[96,32,128]{2,0,1:T(8,128)(2,1)S(1)}, u32[]{:S(2)}, u32[]{:S(2)}) async-start(bf16[96,32,128]{2,0,1:T(8,128)(2,1)} %copy.40), calls=%async_computation | async-start | bytes 1572864 | tf_op jit(solution)/shard_map/all_to_all | solution.py:66
  90.5 59.9 %all-to-all-start.1 = ((bf16[128,32,128]{0,2,1:T(8,128)(2,1)}), bf16[128,32,128]{0,2,1:T(8,128)(2,1)S(1)}, u32[]{:S(2)}, u32[]{:S(2)}) async-start(bf16[128,32,128]{0,2,1:T(8,128)(2,1)} %bitcast.17), calls=%async_computation.1 | async-start | bytes 2097152 | tf_op jit(solution)/shard_map/all_to_all | solution.py:60
  150.4 61.1 %all-to-all-start.2 = ((bf16[128,32,128]{0,2,1:T(8,128)(2,1)}), bf16[128,32,128]{0,2,1:T(8,128)(2,1)}, u32[]{:S(2)}, u32[]{:S(2)}) async-start(bf16[128,32,128]{0,2,1:T(8,128)(2,1)} %bitcast.20), calls=%async_computation.2 | async-start | bytes 2097152 | tf_op jit(solution)/shard_map/all_to_all | solution.py:61
  249.8 18.8 %all-to-all-start.5 = ((f32[16,32,6,1]{0,3,2,1:T(1,128)}), f32[16,32,6,1]{0,3,2,1:T(1,128)S(1)}, u32[]{:S(2)}, u32[]{:S(2)}) async-start(f32[16,32,6,1]{0,3,2,1:T(1,128)} %copy.52), calls=%async_computation.5 | async-start | bytes 196608 | tf_op jit(solution)/shard_map/all_to_all | solution.py:82
  268.6 19.6 %all-to-all-start.3 = ((f32[16,32,6,1]{0,3,2,1:T(1,128)}), f32[16,32,6,1]{0,3,2,1:T(1,128)S(1)}, u32[]{:S(2)}, u32[]{:S(2)}) async-start(f32[16,32,6,1]{0,3,2,1:T(1,128)} %copy.48), calls=%async_computation.3 | async-start | bytes 196608 | tf_op jit(solution)/shard_map/all_to_all | solution.py:89
  288.2 11.0 %all-to-all-start.6 = ((f32[16,1,192]{2,1,0:T(1,128)}), f32[16,1,192]{2,1,0:T(1,128)S(1)}, u32[]{:S(2)}, u32[]{:S(2)}) async-start(f32[16,1,192]{2,1,0:T(1,128)} %reshape.106), calls=%async_computation.6 | async-start | bytes 32768 | tf_op jit(solution)/shard_map/all_to_all | solution.py:81
  299.2 51.5 %all-to-all-start.7 = ((bf16[16,32,6,128]{3,0,2,1:T(8,128)(2,1)}), bf16[16,32,6,128]{3,0,2,1:T(8,128)(2,1)S(1)}, u32[]{:S(2)}, u32[]{:S(2)}) async-start(bf16[16,32,6,128]{3,0,2,1:T(8,128)(2,1)} %copy.56), calls=%async_computation.7 | async-start | bytes 1572864 | tf_op jit(solution)/shard_map/all_to_all | solution.py:74
  350.7 9.9 %all-to-all-start.4 = ((f32[16,1,192]{2,1,0:T(1,128)}), f32[16,1,192]{2,1,0:T(1,128)S(1)}, u32[]{:S(2)}, u32[]{:S(2)}) async-start(f32[16,1,192]{2,1,0:T(1,128)} %reshape.108), calls=%async_computation.4 | async-start | bytes 32768 | tf_op jit(solution)/shard_map/all_to_all | solution.py:88
  360.6 19.1 %all-to-all-start.8 = ((bf16[16,1,6,4096]{3,2,1,0:T(8,128)(2,1)}), bf16[16,1,6,4096]{3,2,1,0:T(8,128)(2,1)}, u32[]{:S(2)}, u32[]{:S(2)}) async-start(bf16[16,1,6,4096]{3,2,1,0:T(8,128)(2,1)} %reshape.103), calls=%async_computation.8 | async-start | bytes 2097152 | tf_op jit(solution)/shard_map/all_to_all | solution.py:73
where the time goes:
time: 385 us; the launch traced here: 383 us
  waiting for transfers between devices  234 us (61%)
  starting transfers between devices  59.2 us (15%)
  matrix products  26.2 us (7%)
  local copies, waits for them, and re-layouts  24.8 us (6%)
  blocking collectives  21.1 us (5%)
  other arithmetic  15.9 us (4%)
    all_to_all x1, waiting for transfers between devices, local(): lax.all_to_all(key, 'seq', split_axis=1, concat_axis=0, tiled=True)  53.5 us
    all_to_all x1, waiting for transfers between devices, local(): lax.all_to_all(value, 'seq', split_axis=1, concat_axis=0, tiled=True)  53.3 us
    all_to_all x1, waiting for transfers between devices, local(): lax.all_to_all(mixed, 'seq', split_axis=1, concat_axis=3, tiled=True)  43 us
    all_to_all x1, waiting for transfers between devices, local(): lax.all_to_all(gathered, 'seq', split_axis=1, concat_axis=0, tiled=True)  42.4 us
    all_gather x1, blocking collectives, local(): gathered = lax.all_gather(chosen, 'blk', axis=0, tiled=True)  21.1 us
    all_to_all x1, starting transfers between devices, local(): lax.all_to_all(gathered, 'seq', split_axis=1, concat_axis=0, tiled=True)  20.8 us
    dot_general x6, matrix products, one_block(): jnp.einsum('rhd,khd->hrk', block, keys, preferred_element_type=jnp.float32)  13.4 us
    all_to_all x1, waiting for transfers between devices, local(): lax.all_to_all(top, 'seq', split_axis=1, concat_axis=3, tiled=True)  13.1 us
  transfers between devices with their start and end apart: 9, of which 9 were waited for; matrix products, arithmetic and copies ran while one was open for 6% of the time, Pallas kernels for 0%

commit v1 on v0

v1 whole, which is shorter than its diff:
```python
import functools
import math

import jax
import jax.numpy as jnp
from jax import lax
from jax.experimental import pallas as pl
from jax.experimental.pallas import tpu as pltpu
from jax.sharding import Mesh, PartitionSpec as P

HD = 128
HEADS = 32
TOK = 128
SLOTS = 6
PAD = 8
CHIPS_Z = 16
NZO = 8
ROWS = HEADS * SLOTS
TAIL = 16
MSG = ROWS + TAIL
SCALE = math.log2(math.e) / math.sqrt(HD)
KEYS = HEADS * TOK
CHUNK = 1024
BF = jnp.bfloat16
F32 = jnp.float32
NT = (((1,), (1,)), ((), ()))
PLANE = ("c", "blk")
VMEM = pl.BlockSpec(memory_space=pltpu.VMEM)
SMEM = pl.BlockSpec(memory_space=pltpu.SMEM)


def iota(shape, dim):
    return lax.broadcasted_iota(jnp.int32, shape, dim)


def choose_body(index_ref, count_ref, query_ref, out_ref):
    row = iota((16, TOK), 0)
    col = iota((16, TOK), 1)
    hot = jnp.zeros((16, TOK), F32)
    for r in range(SLOTS):
        hot = jnp.where((row == r) & (col == index_ref[r]), 1.0, hot)
    rows = jnp.dot(hot.astype(BF), query_ref[...], preferred_element_type=F32)
    count = count_ref[0].astype(F32)
    place = iota((PAD, HD), 0)
    for h in range(HEADS):
        part = rows[:PAD, h * HD:(h + 1) * HD]
        out_ref[h] = jnp.where(place == SLOTS, count, part).astype(BF)


def choose(query, index, counts):
    return pl.pallas_call(
        choose_body,
        out_shape=jax.ShapeDtypeStruct((HEADS, PAD, HD), BF),
        in_specs=[SMEM, SMEM, VMEM],
        out_specs=VMEM,
        name="choose",
    )(index, counts, query)


def split_body(per, key_ref, value_ref, out_ref):
    for h in range(per):
        out_ref[h, :TOK, :] = key_ref[:, h * HD:(h + 1) * HD]
        out_ref[h, TOK:, :] = value_ref[:, h * HD:(h + 1) * HD]


def split_heads(key, value):
    per = 8
    return pl.pallas_call(
        functools.partial(split_body, per),
        grid=(HEADS // per,),
        in_specs=[pl.BlockSpec((TOK, per * HD), lambda i: (0, i))] * 2,
        out_specs=pl.BlockSpec((per, 2 * TOK, HD), lambda i: (i, 0, 0)),
        out_shape=jax.ShapeDtypeStruct((HEADS, 2 * TOK, HD), BF),
        name="split_heads",
    )(key, value)


def compact_body(rows_ref, out_ref, back_ref):
    n = HEADS * PAD
    rows = rows_ref[...].astype(F32).reshape(n, HD).astype(BF)
    down, across = iota((n, n), 0), iota((n, n), 1)
    pick = jnp.where(across == (down // PAD) * PAD + SLOTS, 1.0, 0.0).astype(BF)
    count_col = jnp.dot(pick, rows, preferred_element_type=F32)
    slot_col = iota((n, HD), 0) % PAD
    live_col = (slot_col.astype(F32) < count_col) & (slot_col < SLOTS)
    live_col = jnp.where(live_col, 1.0, 0.0)
    below = jnp.where(across < down, 1.0, 0.0).astype(BF)
    pos_col = jnp.dot(below, live_col.astype(BF), preferred_element_type=F32)
    pos_col = jnp.concatenate([pos_col, pos_col], 1)
    live_two = jnp.concatenate([live_col, live_col], 1)
    back_ref[...] = jnp.where(pos_col == across.astype(F32), live_two, 0.0).astype(BF)
    first = jnp.where(iota((16, HD), 1) == 0, 1.0, 0.0).astype(BF)
    live_row = lax.dot_general(first, live_col.astype(BF), NT, preferred_element_type=F32)
    above = jnp.where(down < across, 1.0, 0.0).astype(BF)
    pos_row = jnp.dot(live_row.astype(BF), above, preferred_element_type=F32)
    pos_row = jnp.broadcast_to(pos_row[:1], (n, n))
    live_row = jnp.broadcast_to(live_row[:1], (n, n))
    move = jnp.where(pos_row == down.astype(F32), live_row, 0.0).astype(BF)
    moved = jnp.dot(move, rows, preferred_element_type=F32)
    out_ref[:ROWS] = moved[:ROWS].astype(BF)
    total = jnp.sum(live_col, axis=0, keepdims=True)
    out_ref[ROWS:] = jnp.broadcast_to(total, (TAIL, HD)).astype(BF)


def compact(rows):
    n = HEADS * PAD
    return pl.pallas_call(
        compact_body,
        out_shape=(jax.ShapeDtypeStruct((MSG, HD), BF), jax.ShapeDtypeStruct((n, n), BF)),
        in_specs=[VMEM],
        out_specs=(VMEM, VMEM),
        name="compact",
    )(rows)


def tail_of(first, second):
    place = iota((TAIL, HD), 0)
    tile = jnp.zeros((TAIL, HD), F32)
    for half, lanes in enumerate((first, second)):
        rest = lanes
        for term in range(3):
            piece = rest.astype(BF).astype(F32)
            rest = rest - piece
            tile = jnp.where(place == 2 * term + half, piece, tile)
    return tile.astype(BF)


def lanes_of(tail):
    tail = tail.astype(F32)
    return tail[0:2] + tail[2:4] + tail[4:6]


def column_to_lanes(column):
    n = column.shape[0]
    full = jnp.broadcast_to(column, (n, HD))
    out = []
    for at in (0, HD):
        size = min(HD, n - at)
        if size <= 0:
            out.append(jnp.zeros((1, HD), F32))
            continue
        diag = iota((size, HD), 0) == iota((size, HD), 1)
        out.append(jnp.sum(jnp.where(diag, full[at:at + size], 0.0), axis=0, keepdims=True))
    return out


def lanes_to_column(lanes):
    out = []
    for half, size in enumerate((HD, ROWS - HD)):
        diag = iota((size, HD), 0) == iota((size, HD), 1)
        full = jnp.broadcast_to(lanes[half:half + 1], (size, HD))
        out.append(jnp.sum(jnp.where(diag, full, 0.0), axis=1, keepdims=True))
    return jnp.concatenate(out, 0)


def attend_rows(group, rows, query_ref, kv_ref, out_ref):
    size = group * rows
    query = query_ref[:, 0, :rows, :].reshape(size, HD)
    per = CHUNK // TOK
    top = mixed = total = None
    for j in range(KEYS // CHUNK):
        keys = kv_ref[j * per:(j + 1) * per, :TOK, :].reshape(CHUNK, HD)
        values = kv_ref[j * per:(j + 1) * per, TOK:, :].reshape(CHUNK, HD)
        scores = lax.dot_general(query, keys, NT, preferred_element_type=F32)
        high = scores[:, :HD]
        for t in range(1, per):
            high = jnp.maximum(high, scores[:, t * HD:(t + 1) * HD])
        high = jnp.broadcast_to(jnp.max(high, axis=1, keepdims=True) * SCALE, (size, HD))
        peak = high if top is None else jnp.maximum(top, high)
        weights, part_total = [], None
        for t in range(per):
            power = jnp.exp2(scores[:, t * HD:(t + 1) * HD] * SCALE - peak)
            part_total = power if part_total is None else part_total + power
            weights.append(power.astype(BF))
        part = jnp.dot(jnp.concatenate(weights, 1), values, preferred_element_type=F32)
        if top is None:
            mixed, total = part, part_total
        else:
            fade = jnp.exp2(top - peak)
            mixed = mixed * fade + part
            total = total * fade + part_total
        top = peak
    total = jnp.sum(total, axis=1, keepdims=True)
    out_ref[:, :rows, :] = (mixed / total).astype(BF).reshape(group, rows, HD)
    level = top[:, :1] + jnp.log2(total)
    for g in range(group):
        out_ref[g, ROWS:, :] = tail_of(*column_to_lanes(level[g * rows:(g + 1) * rows]))


def attend_body(group, side_ref, query_ref, kv_ref, out_ref):
    attend_rows(group, ROWS, query_ref, kv_ref, out_ref)


def attend(side, query, kv):
    group = 2
    work = NZO * ROWS * KEYS * HD * 4
    return pl.pallas_call(
        functools.partial(attend_body, group),
        grid_spec=pltpu.PrefetchScalarGridSpec(
            num_scalar_prefetch=1,
            grid=(NZO // group,),
            in_specs=[
                pl.BlockSpec((group, 1, MSG, HD), lambda i, side: (i, side[0], 0, 0)),
                pl.BlockSpec((HEADS, 2 * TOK, HD), lambda i, side: (0, 0, 0)),
            ],
            out_specs=pl.BlockSpec((group, MSG, HD), lambda i, side: (i, 0, 0)),
        ),
        out_shape=jax.ShapeDtypeStruct((NZO, MSG, HD), BF),
        compiler_params=pltpu.CompilerParams(vmem_limit_bytes=40 * 2**20),
        cost_estimate=pl.CostEstimate(
            flops=2 * work, bytes_accessed=6 * 2**20, transcendentals=NZO * ROWS * KEYS
        ),
        name="attend",
    )(side, query, kv)


def pair_body(group, own_ref, other_ref, out_ref):
    for g in range(group):
        a, b = lanes_of(own_ref[g, ROWS:, :]), lanes_of(other_ref[g, ROWS:, :])
        peak = jnp.maximum(a, b)
        wa, wb = jnp.exp2(a - peak), jnp.exp2(b - peak)
        both = wa + wb
        level = peak + jnp.log2(both)
        ca, cb = lanes_to_column(wa / both), lanes_to_column(wb / both)
        out_ref[g, :ROWS, :] = (
            own_ref[g, :ROWS, :].astype(F32) * ca + other_ref[g, :ROWS, :].astype(F32) * cb
        ).astype(BF)
        out_ref[g, ROWS:, :] = tail_of(level[0:1], level[1:2])


def merge_pair(own, other):
    group = 4
    spec = pl.BlockSpec((group, MSG, HD), lambda i: (i, 0, 0))
    return pl.pallas_call(
        functools.partial(pair_body, group),
        grid=(NZO // group,),
        in_specs=[spec, spec],
        out_specs=spec,
        out_shape=jax.ShapeDtypeStruct((NZO, MSG, HD), BF),
        name="merge_pair",
    )(own, other)


def finish_body(parts_ref, live_ref, back_ref, out_ref):
    levels = [lanes_of(parts_ref[i, ROWS:, :]) for i in range(NZO)]
    peak = functools.reduce(jnp.maximum, levels)
    weights = [jnp.exp2(level - peak) for level in levels]
    both = functools.reduce(jnp.add, weights)
    mixed = None
    for i in range(NZO):
        column = lanes_to_column(weights[i] / both)
        part = parts_ref[i, :ROWS, :].astype(F32) * column
        mixed = part if mixed is None else mixed + part
    count = live_ref[ROWS:, :].astype(F32)[:1]
    alive = iota((ROWS, HD), 0).astype(F32) < count
    mixed = jnp.where(alive, mixed, 0.0).astype(BF)
    rows = jnp.dot(back_ref[:, :ROWS], mixed, preferred_element_type=F32)
    out_ref[...] = rows.reshape(HEADS, PAD, HD).astype(BF)


def finish(parts, live, back):
    return pl.pallas_call(
        finish_body,
        out_shape=jax.ShapeDtypeStruct((HEADS, PAD, HD), BF),
        in_specs=[VMEM, VMEM, VMEM],
        out_specs=VMEM,
        name="finish",
    )(parts, live, back)


def gate_body(count_ref, rows_ref, gate_ref, out_ref):
    alive = iota((PAD, HD), 0) < count_ref[0]
    for h in range(HEADS):
        gated = gate_ref[:, h * HD:(h + 1) * HD] * rows_ref[h].astype(F32)
        gated = jnp.where(alive, gated, 0.0)
        out_ref[:, h * HD:(h + 1) * HD] = gated[:SLOTS].astype(BF)


def apply_gate(counts, rows, gate):
    return pl.pallas_call(
        gate_body,
        out_shape=jax.ShapeDtypeStruct((SLOTS, HEADS * HD), BF),
        in_specs=[SMEM, VMEM, VMEM],
        out_specs=VMEM,
        name="apply_gate",
    )(counts, rows, gate)


def after(value, token):
    return lax.optimization_barrier((value, token))[0]


def swap(x, axes):
    return lax.all_to_all(x, axes, split_axis=0, concat_axis=0, tiled=True)


def local(query, key, value, index, counts, timestep, gate_table):
    side = lax.axis_index("zi").astype(jnp.int32).reshape(1)
    mine = choose(query, index, counts)
    kv = split_heads(key, value)
    plane_rows = swap(mine, PLANE)
    kv = swap(after(kv, plane_rows), PLANE)
    live, back = compact(plane_rows)
    rows = lax.all_gather(live, ("zo", "zi"), axis=0, tiled=False)
    rows = rows.reshape(NZO, 2, MSG, HD)
    away = attend(1 - side, rows, kv)
    arrived = lax.ppermute(away, "zi", [(0, 1), (1, 0)])
    own = attend(side, rows, kv)
    merged = merge_pair(own, arrived)
    parts = swap(merged, "zo")
    sent = finish(parts, live, back)
    heads = swap(sent, PLANE)
    gate = lax.dynamic_slice_in_dim(gate_table, timestep[0], 1, 0)
    return apply_gate(counts, heads, gate)


def solution(mesh):
    blk = mesh.shape["blk"]
    inner = Mesh(mesh.devices.reshape(NZO, 2, 2, blk), ("zo", "zi", "c", "blk"))
    every = ("zo", "zi", "c", "blk")
    in_specs = (
        P(every, None),
        P(every, None),
        P(every, None),
        P(every),
        P(every),
        P(),
        P(),
    )
    return jax.shard_map(
        local, mesh=inner, in_specs=in_specs, out_specs=P(every, None), check_vma=False
    )
```

time: 385 us -> 147 us (0.38)
  waiting for transfers between devices: 234 us -> 27.1 us
  Pallas kernels: 0 us -> 35 us
  matrix products: 26.2 us -> 0 us
  local copies, waits for them, and re-layouts: 24.8 us -> 5.3 us
  starting transfers between devices: 59.2 us -> 42.4 us
  other arithmetic: 15.9 us -> 0 us
  blocking collectives: 21.1 us -> 34.9 us
    all_to_all x9 -> x4, waiting for transfers between devices: 234 us -> 27.1 us  [swap(): return lax.all_to_all(x, axes, split_axis=0, concat_axis=0, tiled=True)]
    pallas_call x0 -> x8, Pallas kernels: none -> 35 us  [the longest x2 20.2 us: attend(): pl.pallas_call(functools.partial(attend_body, group), grid_spec=pltpu.Pre...]
    dot_general x12 -> x0, matrix products: 26.2 us -> none  [the longest x6 13.4 us: one_block(): jnp.einsum('rhd,khd->hrk', block, keys, preferred_element_type=jnp.float32)]
    all_to_all x9 -> x4, starting transfers between devices: 59.2 us -> 40.5 us  [swap(): return lax.all_to_all(x, axes, split_axis=0, concat_axis=0, tiled=True)]
    all_gather x1, blocking collectives: 21.1 us -> 34.9 us  [local(): rows = lax.all_gather(live, ('zo', 'zi'), axis=0, tiled=False)]
    reduce_sum x8 -> x0, other arithmetic: 11.5 us -> none  [the longest x6 9.05 us: one_block(): total = jnp.sum(powers, axis=2)]
    all_to_all x11 -> x0, local copies, waits for them, and re-layouts: 7.14 us -> none  [the longest x3 2.44 us: local(): lax.all_to_all(gathered, 'seq', split_axis=1, concat_axis=0, tiled=True)]
    another operation x7 -> x0, local copies, waits for them, and re-layouts: 6.52 us -> none  [the longest x2 3.11 us: local(): mixed = mixed.reshape(blk_size, seq_size, slots, head_width)]
  transfers between devices with their start and end apart: 9 -> 5, of which waited for: 9 -> 3; matrix products, arithmetic and copies ran while one was open for 6% -> 0% of each run, Pallas kernels for 0% -> 11%
where the time goes in v1:
time: 147 us; the launch traced here: 146 us
  starting transfers between devices  42.4 us (29%)
  Pallas kernels  35 us (24%)
  blocking collectives  34.9 us (24%)
  waiting for transfers between devices  27.1 us (18%)
  local copies, waits for them, and re-layouts  5.3 us (4%)
  between operations  1.48 us (1%)
    all_to_all x4, starting transfers between devices, swap(): return lax.all_to_all(x, axes, split_axis=0, concat_axis=0, tiled=True)  40.5 us
    all_gather x1, blocking collectives, local(): rows = lax.all_gather(live, ('zo', 'zi'), axis=0, tiled=False)  34.9 us
    all_to_all x4, waiting for transfers between devices, swap(): return lax.all_to_all(x, axes, split_axis=0, concat_axis=0, tiled=True)  27.1 us
    pallas_call x2, Pallas kernels, attend(): pl.pallas_call(functools.partial(attend_body, group), grid_spec=pltpu.Pre...  20.2 us
    unnamed x16, local copies, waits for them, and re-layouts  4.67 us
    pallas_call x1, Pallas kernels, split_heads(): pl.pallas_call(functools.partial(split_body, per), grid=(HEADS // per,),...  3.91 us
  transfers between devices with their start and end apart: 5, of which 3 were waited for; matrix products, arithmetic and copies ran while one was open for 0% of the time, Pallas kernels for 11%

profile of v1, /device:TPU:1, one launch (start us, length us, event | category | flops | bytes accessed | tf_op | source)
XLA Modules:
  0.0 146.2 jit_solution(10438969137415445270)
XLA Ops:
  0.0 0.0 copy-start
  0.7 2.1 %choose.1 = bf16[32,8,128]{2,1,0:T(8,128)(2,1)} custom-call(s32[6]{0:T(128)} %index_ref.1, s32[1]{0:T(128)S(6)} %copy.8.count_ref, bf16[128,4096]{1,0:T(8,128)(2,1)} %query_ref.1), custom_call_target="tpu_custom_call" | custom-call | tf_op jit(solution)/shard_map/choose/pallas_call | solution.py:51
  2.9 10.5 %all-to-all-start = ((bf16[32,8,128]{2,1,0:T(8,128)(2,1)}), bf16[32,8,128]{2,1,0:T(8,128)(2,1)S(1)}, u32[]{:S(2)}, u32[]{:S(2)}) async-start(bf16[32,8,128]{2,1,0:T(8,128)(2,1)} %choose.1), calls=%async_computation | async-start | bytes 131072 | tf_op jit(solution)/shard_map/all_to_all | solution.py:294
  13.3 3.9 %split_heads.1 = bf16[32,256,128]{2,1,0:T(8,128)(2,1)} custom-call(bf16[128,4096]{1,0:T(8,128)(2,1)} %key_ref.1, bf16[128,4096]{1,0:T(8,128)(2,1)} %value_ref.1), custom_call_target="tpu_custom_call" | custom-call | tf_op jit(solution)/shard_map/split_heads/pallas_call | solution.py:68
  17.3 3.2 %all-to-all-done.rows_ref = bf16[32,8,128]{2,1,0:T(8,128)(2,1)S(1)} async-done(((bf16[32,8,128]{2,1,0:T(8,128)(2,1)}), bf16[32,8,128]{2,1,0:T(8,128)(2,1)S(1)}, u32[]{:S(2)}, u32[]{:S(2)}) %all-to-all-start) | async-done | bytes 65568 | tf_op jit(solution)/shard_map/all_to_all | solution.py:294
  20.5 0.0 copy-start.6
  20.5 0.6 copy-done.6
  21.1 4.3 %all-to-all-start.1 = ((bf16[32,256,128]{2,1,0:T(8,128)(2,1)}), bf16[32,256,128]{2,1,0:T(8,128)(2,1)S(1)}, u32[]{:S(2)}, u32[]{:S(2)}) async-start(bf16[32,256,128]{2,1,0:T(8,128)(2,1)} %split_heads.1), calls=%async_computation.1 | async-start | bytes 4194304 | tf_op jit(solution)/shard_map/all_to_all | solution.py:294
  25.4 2.0 %compact.1 = (bf16[208,128]{1,0:T(8,128)(2,1)}, bf16[256,256]{1,0:T(8,128)(2,1)}) custom-call(bf16[32,8,128]{2,1,0:T(8,128)(2,1)} %copy-done.6), custom_call_target="tpu_custom_call" | custom-call | tf_op jit(solution)/shard_map/compact/pallas_call | solution.py:107
  27.4 34.9 %all-gather = bf16[3328,128]{1,0:T(8,128)(2,1)} all-gather(bf16[208,128]{1,0:T(8,128)(2,1)} %get-tuple-element.8.live_ref), channel_id=2, replica_groups=mesh['zo'=8,'zi'=2,'c'=2,'blk'=16] {'zo','zi'}, dimensions={0}, use_global_device_ids=true | all-gather | bytes 905216 | tf_op jit(solution)/shard_map/all_gather | solution.py:304
  62.4 0.0 all-to-all-done.1.kv_ref
  62.4 0.0 copy-start.1
  62.4 1.2 copy-done.1
  63.5 0.0 copy-start.2
  63.5 10.1 %attend.3 = bf16[8,208,128]{2,1,0:T(8,128)(2,1)S(1)} custom-call(s32[1]{0:T(128)S(6)} %sub.3.side_ref, bf16[8,2,208,128]{3,2,1,0:T(8,128)(2,1)S(1)} %bitcast.6, bf16[32,256,128]{2,1,0:T(8,128)(2,1)S(1)} %all-to-all-done.1.kv_ref), custom_call_target="tpu_custom_call" | custom-call | flops 6442450944 | bytes 6291456 | tf_op jit(solution)/shard_map/attend/pallas_call | solution.py:197
  73.6 1.9 %collective-permute-start = (bf16[8,208,128]{2,1,0:T(8,128)(2,1)S(1)}, bf16[8,208,128]{2,1,0:T(8,128)(2,1)S(1)}, u32[]{:S(2)}, u32[]{:S(2)}) collective-permute-start(bf16[8,208,128]{2,1,0:T(8,128)(2,1)S(1)} %attend.3), channel_id=1, source_target_pairs={{0,32},{32,0},{1,33},{33,1},{2,34},{34,2},{3,35},{35,3},{4,36},{36... | collective-permute-start | bytes 1277960 | tf_op jit(solution)/shard_map/ppermute | solution.py:307
  75.6 0.0 copy-done.2
  75.6 10.1 %attend.2.own_ref = bf16[8,208,128]{2,1,0:T(8,128)(2,1)S(1)} custom-call(s32[1]{0:T(128)} %bitcast.side_ref, bf16[8,2,208,128]{3,2,1,0:T(8,128)(2,1)S(1)} %bitcast.7, bf16[32,256,128]{2,1,0:T(8,128)(2,1)S(1)} %all-to-all-done.1.kv_ref), custom_call_target="tpu_custom_call" | custom-call | flops 6442450944 | bytes 6291456 | tf_op jit(solution)/shard_map/attend/pallas_call | solution.py:197
  85.7 0.0 copy-start.3
  85.7 0.7 copy-done.3
  86.4 0.0 collective-permute-done.other_ref
  86.4 0.0 copy-start.5
  86.4 0.8 copy-done.5
  87.2 2.8 %merge_pair.1 = bf16[8,208,128]{2,1,0:T(8,128)(2,1)} custom-call(bf16[8,208,128]{2,1,0:T(8,128)(2,1)} %copy-done.3, bf16[8,208,128]{2,1,0:T(8,128)(2,1)} %copy-done.5), custom_call_target="tpu_custom_call" | custom-call | tf_op jit(solution)/shard_map/merge_pair/pallas_call | solution.py:234
  90.0 7.3 %all-to-all-start.2 = ((bf16[8,208,128]{2,1,0:T(8,128)(2,1)}), bf16[8,208,128]{2,1,0:T(8,128)(2,1)S(1)}, u32[]{:S(2)}, u32[]{:S(2)}) async-start(bf16[8,208,128]{2,1,0:T(8,128)(2,1)} %merge_pair.1), calls=%async_computation.2 | async-start | bytes 851968 | tf_op jit(solution)/shard_map/all_to_all | solution.py:294
  98.0 17.4 %all-to-all-done.2.parts_ref = bf16[8,208,128]{2,1,0:T(8,128)(2,1)S(1)} async-done(((bf16[8,208,128]{2,1,0:T(8,128)(2,1)}), bf16[8,208,128]{2,1,0:T(8,128)(2,1)S(1)}, u32[]{:S(2)}, u32[]{:S(2)}) %all-to-all-start.2) | async-done | bytes 426016 | tf_op jit(solution)/shard_map/all_to_all | solution.py:294
  115.4 0.0 copy-start.4
  115.4 0.8 copy-done.4
  116.2 2.4 %finish.1 = bf16[32,8,128]{2,1,0:T(8,128)(2,1)} custom-call(bf16[8,208,128]{2,1,0:T(8,128)(2,1)} %copy-done.4, bf16[208,128]{1,0:T(8,128)(2,1)} %get-tuple-element.8.live_ref, bf16[256,256]{1,0:T(8,128)(2,1)} %get-tuple-element.10.back_ref), custom_call_target="tpu_custom_call" | custom-call | tf_op jit(solution)/shard_map/finish/pallas_call | solution.py:262
  118.6 18.4 %all-to-all-start.3 = ((bf16[32,8,128]{2,1,0:T(8,128)(2,1)}), bf16[32,8,128]{2,1,0:T(8,128)(2,1)S(1)}, u32[]{:S(2)}, u32[]{:S(2)}) async-start(bf16[32,8,128]{2,1,0:T(8,128)(2,1)} %finish.1), calls=%async_computation.3 | async-start | bytes 131072 | tf_op jit(solution)/shard_map/all_to_all | solution.py:294
  137.0 0.0 copy-done
  137.0 0.6 constant_dynamic-slice_fusion.gate_ref
  137.6 6.5 %all-to-all-done.3.rows_ref = bf16[32,8,128]{2,1,0:T(8,128)(2,1)S(1)} async-done(((bf16[32,8,128]{2,1,0:T(8,128)(2,1)}), bf16[32,8,128]{2,1,0:T(8,128)(2,1)S(1)}, u32[]{:S(2)}, u32[]{:S(2)}) %all-to-all-start.3) | async-done | bytes 65568 | tf_op jit(solution)/shard_map/all_to_all | solution.py:294
  144.1 0.0 copy-start.7
  144.1 0.6 copy-done.7
  144.7 1.5 %apply_gate.1 = bf16[6,4096]{1,0:T(8,128)(2,1)} custom-call(s32[1]{0:T(128)S(6)} %copy.8.count_ref, bf16[32,8,128]{2,1,0:T(8,128)(2,1)} %copy-done.7, f32[1,4096]{1,0:T(1,128)} %constant_dynamic-slice_fusion.gate_ref), custom_call_target="tpu_custom_call" | custom-call | tf_op jit(solution)/shard_map/apply_gate/pallas_call | solution.py:280
Async XLA Ops:
  0.0 137.0 %copy-start = (f32[50,4096]{1,0:T(8,128)S(1)}, f32[50,4096]{1,0:T(8,128)}, u32[]{:S(2)}) copy-start(f32[50,4096]{1,0:T(8,128)} %param.13) | copy-start | bytes 2457604
  2.9 17.6 %all-to-all-start = ((bf16[32,8,128]{2,1,0:T(8,128)(2,1)}), bf16[32,8,128]{2,1,0:T(8,128)(2,1)S(1)}, u32[]{:S(2)}, u32[]{:S(2)}) async-start(bf16[32,8,128]{2,1,0:T(8,128)(2,1)} %choose.1), calls=%async_computation | async-start | bytes 131072 | tf_op jit(solution)/shard_map/all_to_all | solution.py:294
  20.5 0.6 copy-start.6
  21.1 41.3 %all-to-all-start.1 = ((bf16[32,256,128]{2,1,0:T(8,128)(2,1)}), bf16[32,256,128]{2,1,0:T(8,128)(2,1)S(1)}, u32[]{:S(2)}, u32[]{:S(2)}) async-start(bf16[32,256,128]{2,1,0:T(8,128)(2,1)} %split_heads.1), calls=%async_computation.1 | async-start | bytes 4194304 | tf_op jit(solution)/shard_map/all_to_all | solution.py:294
  62.4 1.2 copy-start.1
  63.5 12.0 %copy-start.2 = (bf16[3328,128]{1,0:T(8,128)(2,1)S(1)}, bf16[3328,128]{1,0:T(8,128)(2,1)}, u32[]{:S(2)}) copy-start(bf16[3328,128]{1,0:T(8,128)(2,1)} %all-gather) | copy-start | bytes 2555908
  73.6 12.8 %collective-permute-start = (bf16[8,208,128]{2,1,0:T(8,128)(2,1)S(1)}, bf16[8,208,128]{2,1,0:T(8,128)(2,1)S(1)}, u32[]{:S(2)}, u32[]{:S(2)}) collective-permute-start(bf16[8,208,128]{2,1,0:T(8,128)(2,1)S(1)} %attend.3), channel_id=1, source_target_pairs={{0,32},{32,0},{1,33},{33,1},{2,34},{34,2},{3,35},{35,3},{4,36},{36... | collective-permute-start | bytes 1277960 | tf_op jit(solution)/shard_map/ppermute | solution.py:307
  85.7 0.8 copy-start.3
  86.4 0.8 copy-start.5
  90.0 25.4 %all-to-all-start.2 = ((bf16[8,208,128]{2,1,0:T(8,128)(2,1)}), bf16[8,208,128]{2,1,0:T(8,128)(2,1)S(1)}, u32[]{:S(2)}, u32[]{:S(2)}) async-start(bf16[8,208,128]{2,1,0:T(8,128)(2,1)} %merge_pair.1), calls=%async_computation.2 | async-start | bytes 851968 | tf_op jit(solution)/shard_map/all_to_all | solution.py:294
  115.4 0.8 copy-start.4
  118.6 25.5 %all-to-all-start.3 = ((bf16[32,8,128]{2,1,0:T(8,128)(2,1)}), bf16[32,8,128]{2,1,0:T(8,128)(2,1)S(1)}, u32[]{:S(2)}, u32[]{:S(2)}) async-start(bf16[32,8,128]{2,1,0:T(8,128)(2,1)} %finish.1), calls=%async_computation.3 | async-start | bytes 131072 | tf_op jit(solution)/shard_map/all_to_all | solution.py:294
  144.1 0.6 copy-start.7

commit v2 on v1

--- a/solution.py
+++ b/solution.py
@@ -18,6 +18,7 @@
 ROWS = HEADS * SLOTS
 TAIL = 16
 MSG = ROWS + TAIL
+TIERS = (128, 144, ROWS)
 SCALE = math.log2(math.e) / math.sqrt(HD)
 KEYS = HEADS * TOK
 CHUNK = 1024
@@ -25,6 +26,7 @@
 F32 = jnp.float32
 NT = (((1,), (1,)), ((), ()))
 PLANE = ("c", "blk")
+SMALL = pltpu.CompilerParams(vmem_limit_bytes=12 * 2**20)
 VMEM = pl.BlockSpec(memory_space=pltpu.VMEM)
 SMEM = pl.BlockSpec(memory_space=pltpu.SMEM)
 
@@ -53,6 +55,7 @@
         out_shape=jax.ShapeDtypeStruct((HEADS, PAD, HD), BF),
         in_specs=[SMEM, SMEM, VMEM],
         out_specs=VMEM,
+        compiler_params=SMALL,
         name="choose",
     )(index, counts, query)
 
@@ -71,6 +74,7 @@
         in_specs=[pl.BlockSpec((TOK, per * HD), lambda i: (0, i))] * 2,
         out_specs=pl.BlockSpec((per, 2 * TOK, HD), lambda i: (i, 0, 0)),
         out_shape=jax.ShapeDtypeStruct((HEADS, 2 * TOK, HD), BF),
+        compiler_params=SMALL,
         name="split_heads",
     )(key, value)
 
@@ -109,6 +113,7 @@
         out_shape=(jax.ShapeDtypeStruct((MSG, HD), BF), jax.ShapeDtypeStruct((n, n), BF)),
         in_specs=[VMEM],
         out_specs=(VMEM, VMEM),
+        compiler_params=SMALL,
         name="compact",
     )(rows)
 
@@ -144,9 +149,11 @@
     return out
 
 
-def lanes_to_column(lanes):
+def lanes_to_column(lanes, rows):
     out = []
-    for half, size in enumerate((HD, ROWS - HD)):
+    for half, size in enumerate((min(rows, HD), rows - HD)):
+        if size <= 0:
+            continue
         diag = iota((size, HD), 0) == iota((size, HD), 1)
         full = jnp.broadcast_to(lanes[half:half + 1], (size, HD))
         out.append(jnp.sum(jnp.where(diag, full, 0.0), axis=1, keepdims=True))
@@ -184,18 +191,18 @@
     out_ref[:, :rows, :] = (mixed / total).astype(BF).reshape(group, rows, HD)
     level = top[:, :1] + jnp.log2(total)
     for g in range(group):
-        out_ref[g, ROWS:, :] = tail_of(*column_to_lanes(level[g * rows:(g + 1) * rows]))
-
-
-def attend_body(group, side_ref, query_ref, kv_ref, out_ref):
-    attend_rows(group, ROWS, query_ref, kv_ref, out_ref)
-
-
-def attend(side, query, kv):
-    group = 2
-    work = NZO * ROWS * KEYS * HD * 4
-    return pl.pallas_call(
-        functools.partial(attend_body, group),
+        out_ref[g, rows:, :] = tail_of(*column_to_lanes(level[g * rows:(g + 1) * rows]))
+
+
+def attend_body(group, rows, side_ref, query_ref, kv_ref, out_ref):
+    attend_rows(group, rows, query_ref, kv_ref, out_ref)
+
+
+def attend(rows, side, query, kv):
+    group = 8 if rows == TIERS[0] else 4
+    work = NZO * rows * KEYS * HD * 4
+    return pl.pallas_call(
+        functools.partial(attend_body, group, rows),
         grid_spec=pltpu.PrefetchScalarGridSpec(
             num_scalar_prefetch=1,
             grid=(NZO // group,),
@@ -203,67 +210,70 @@
                 pl.BlockSpec((group, 1, MSG, HD), lambda i, side: (i, side[0], 0, 0)),
                 pl.BlockSpec((HEADS, 2 * TOK, HD), lambda i, side: (0, 0, 0)),
             ],
-            out_specs=pl.BlockSpec((group, MSG, HD), lambda i, side: (i, 0, 0)),
+            out_specs=pl.BlockSpec((group, rows + TAIL, HD), lambda i, side: (i, 0, 0)),
         ),
-        out_shape=jax.ShapeDtypeStruct((NZO, MSG, HD), BF),
+        out_shape=jax.ShapeDtypeStruct((NZO, rows + TAIL, HD), BF),
         compiler_params=pltpu.CompilerParams(vmem_limit_bytes=40 * 2**20),
         cost_estimate=pl.CostEstimate(
-            flops=2 * work, bytes_accessed=6 * 2**20, transcendentals=NZO * ROWS * KEYS
+            flops=2 * work, bytes_accessed=6 * 2**20, transcendentals=NZO * rows * KEYS
         ),
         name="attend",
     )(side, query, kv)
 
 
-def pair_body(group, own_ref, other_ref, out_ref):
+def pair_body(group, rows, own_ref, other_ref, out_ref):
     for g in range(group):
-        a, b = lanes_of(own_ref[g, ROWS:, :]), lanes_of(other_ref[g, ROWS:, :])
+        a, b = lanes_of(own_ref[g, rows:, :]), lanes_of(other_ref[g, rows:, :])
         peak = jnp.maximum(a, b)
         wa, wb = jnp.exp2(a - peak), jnp.exp2(b - peak)
         both = wa + wb
         level = peak + jnp.log2(both)
-        ca, cb = lanes_to_column(wa / both), lanes_to_column(wb / both)
-        out_ref[g, :ROWS, :] = (
-            own_ref[g, :ROWS, :].astype(F32) * ca + other_ref[g, :ROWS, :].astype(F32) * cb
+        ca, cb = lanes_to_column(wa / both, rows), lanes_to_column(wb / both, rows)
+        out_ref[g, :rows, :] = (
+            own_ref[g, :rows, :].astype(F32) * ca + other_ref[g, :rows, :].astype(F32) * cb
         ).astype(BF)
-        out_ref[g, ROWS:, :] = tail_of(level[0:1], level[1:2])
+        out_ref[g, rows:, :] = tail_of(level[0:1], level[1:2])
 
 
 def merge_pair(own, other):
     group = 4
-    spec = pl.BlockSpec((group, MSG, HD), lambda i: (i, 0, 0))
-    return pl.pallas_call(
-        functools.partial(pair_body, group),
+    msg = own.shape[1]
+    spec = pl.BlockSpec((group, msg, HD), lambda i: (i, 0, 0))
+    return pl.pallas_call(
+        functools.partial(pair_body, group, msg - TAIL),
         grid=(NZO // group,),
         in_specs=[spec, spec],
         out_specs=spec,
-        out_shape=jax.ShapeDtypeStruct((NZO, MSG, HD), BF),
+        out_shape=jax.ShapeDtypeStruct((NZO, msg, HD), BF),
+        compiler_params=SMALL,
         name="merge_pair",
     )(own, other)
 
 
-def finish_body(parts_ref, live_ref, back_ref, out_ref):
-    levels = [lanes_of(parts_ref[i, ROWS:, :]) for i in range(NZO)]
+def finish_body(rows, parts_ref, live_ref, back_ref, out_ref):
+    levels = [lanes_of(parts_ref[i, rows:, :]) for i in range(NZO)]
     peak = functools.reduce(jnp.maximum, levels)
     weights = [jnp.exp2(level - peak) for level in levels]
     both = functools.reduce(jnp.add, weights)
     mixed = None
     for i in range(NZO):
-        column = lanes_to_column(weights[i] / both)
-        part = parts_ref[i, :ROWS, :].astype(F32) * column
+        column = lanes_to_column(weights[i] / both, rows)
+        part = parts_ref[i, :rows, :].astype(F32) * column
         mixed = part if mixed is None else mixed + part
     count = live_ref[ROWS:, :].astype(F32)[:1]
-    alive = iota((ROWS, HD), 0).astype(F32) < count
+    alive = iota((rows, HD), 0).astype(F32) < count
     mixed = jnp.where(alive, mixed, 0.0).astype(BF)
-    rows = jnp.dot(back_ref[:, :ROWS], mixed, preferred_element_type=F32)
-    out_ref[...] = rows.reshape(HEADS, PAD, HD).astype(BF)
+    placed = jnp.dot(back_ref[:, :rows], mixed, preferred_element_type=F32)
+    out_ref[...] = placed.reshape(HEADS, PAD, HD).astype(BF)
 
 
 def finish(parts, live, back):
     return pl.pallas_call(
-        finish_body,
+        functools.partial(finish_body, parts.shape[1] - TAIL),
         out_shape=jax.ShapeDtypeStruct((HEADS, PAD, HD), BF),
         in_specs=[VMEM, VMEM, VMEM],
         out_specs=VMEM,
+        compiler_params=SMALL,
         name="finish",
     )(parts, live, back)
 
@@ -282,6 +292,7 @@
         out_shape=jax.ShapeDtypeStruct((SLOTS, HEADS * HD), BF),
         in_specs=[SMEM, VMEM, VMEM],
         out_specs=VMEM,
+        compiler_params=SMALL,
         name="apply_gate",
     )(counts, rows, gate)
 
@@ -292,6 +303,15 @@
 
 def swap(x, axes):
     return lax.all_to_all(x, axes, split_axis=0, concat_axis=0, tiled=True)
+
+
+def late(size, side, rows, kv, live, back):
+    away = attend(size, 1 - side, rows, kv)
+    arrived = lax.ppermute(away, "zi", [(0, 1), (1, 0)])
+    own = attend(size, side, rows, kv)
+    merged = merge_pair(own, arrived)
+    parts = swap(merged, "zo")
+    return finish(parts, live, back)
 
 
 def local(query, key, value, index, counts, timestep, gate_table):
@@ -303,12 +323,9 @@
     live, back = compact(plane_rows)
     rows = lax.all_gather(live, ("zo", "zi"), axis=0, tiled=False)
     rows = rows.reshape(NZO, 2, MSG, HD)
-    away = attend(1 - side, rows, kv)
-    arrived = lax.ppermute(away, "zi", [(0, 1), (1, 0)])
-    own = attend(side, rows, kv)
-    merged = merge_pair(own, arrived)
-    parts = swap(merged, "zo")
-    sent = finish(parts, live, back)
+    most = jnp.max(rows[:, :, ROWS, 0].astype(F32))
+    tier = sum((most > limit).astype(jnp.int32) for limit in TIERS[:-1])
+    sent = lax.switch(tier, [functools.partial(late, n) for n in TIERS], side, rows, kv, live, back)
     heads = swap(sent, PLANE)
     gate = lax.dynamic_slice_in_dim(gate_table, timestep[0], 1, 0)
     return apply_gate(counts, heads, gate)

time: 147 us -> 126 us (0.86)
  blocking collectives: 34.9 us -> 57.1 us
  waiting for transfers between devices: 27.1 us -> 9.67 us
  Pallas kernels: 35 us -> 18.7 us
  starting transfers between devices: 42.4 us -> 31.5 us
    all_to_all x0 -> x1, blocking collectives: none -> 23.2 us  [swap(): return lax.all_to_all(x, axes, split_axis=0, concat_axis=0, tiled=True)]
    all_to_all x4 -> x3, waiting for transfers between devices: 27.1 us -> 9.66 us  [swap(): return lax.all_to_all(x, axes, split_axis=0, concat_axis=0, tiled=True)]
    pallas_call x4, Pallas kernels: 25.4 us -> 13.9 us  [the longest x2 12.4 us: attend(): pl.pallas_call(functools.partial(attend_body, group, rows), grid_spec=plt...]
    all_to_all x4 -> x3, starting transfers between devices: 40.5 us -> 29.4 us  [swap(): return lax.all_to_all(x, axes, split_axis=0, concat_axis=0, tiled=True)]
    pallas_call x1, Pallas kernels: 3.91 us -> 2.09 us  [split_heads(): pl.pallas_call(functools.partial(split_body, per), grid=(HEADS // per,),...]
    unnamed x16 -> x12, local copies, waits for them, and re-layouts: 4.67 us -> 5.23 us
  transfers between devices with their start and end apart: 5 -> 4, of which waited for: 3 -> 2; matrix products, arithmetic and copies ran while one was open for 0% -> 1% of each run, Pallas kernels for 11% -> 7%
where the time goes in v2:
time: 126 us
  blocking collectives  57.1 us (45%)
  starting transfers between devices  31.5 us (25%)
  Pallas kernels  18.7 us (15%)
  waiting for transfers between devices  9.67 us (8%)
  local copies, waits for them, and re-layouts  5.25 us (4%)
  between operations  2.78 us (2%)
    all_gather x1, blocking collectives, local(): rows = lax.all_gather(live, ('zo', 'zi'), axis=0, tiled=False)  33.9 us
    all_to_all x3, starting transfers between devices, swap(): return lax.all_to_all(x, axes, split_axis=0, concat_axis=0, tiled=True)  29.4 us
    all_to_all x1, blocking collectives, swap(): return lax.all_to_all(x, axes, split_axis=0, concat_axis=0, tiled=True)  23.2 us
    pallas_call x2, Pallas kernels, attend(): pl.pallas_call(functools.partial(attend_body, group, rows), grid_spec=plt...  12.4 us
    all_to_all x3, waiting for transfers between devices, swap(): return lax.all_to_all(x, axes, split_axis=0, concat_axis=0, tiled=True)  9.66 us
    unnamed x12, local copies, waits for them, and re-layouts  5.23 us
  transfers between devices with their start and end apart: 4, of which 2 were waited for; matrix products, arithmetic and copies ran while one was open for 1% of the time, Pallas kernels for 7%

profile of v2, /device:TPU:1, one launch (start us, length us, event | category | flops | bytes accessed | tf_op | source)
XLA Modules:
  0.0 125.7 jit_solution(884317403098301550)
XLA Ops:
  0.0 0.0 copy-start
  0.7 0.0 copy-start.1
  0.7 1.2 copy-done.1
  2.0 0.0 copy-start.4
  2.0 0.7 copy-done.4
  2.6 1.4 %choose.1 = bf16[32,8,128]{2,1,0:T(8,128)(2,1)} custom-call(s32[6]{0:T(128)S(1)} %copy-done.4, s32[1]{0:T(128)S(6)} %copy.11.count_ref, bf16[128,4096]{1,0:T(8,128)(2,1)S(1)} %copy-done.1), custom_call_target="tpu_custom_call" | custom-call | tf_op jit(solution)/shard_map/choose/pallas_call | solution.py:53
  4.0 10.5 %all-to-all-start.3 = ((bf16[32,8,128]{2,1,0:T(8,128)(2,1)}), bf16[32,8,128]{2,1,0:T(8,128)(2,1)S(1)}, u32[]{:S(2)}, u32[]{:S(2)}) async-start(bf16[32,8,128]{2,1,0:T(8,128)(2,1)} %choose.1), calls=%async_computation.3 | async-start | bytes 131072 | tf_op jit(solution)/shard_map/all_to_all | solution.py:305
  14.5 0.0 copy-start.2
  14.5 1.2 copy-done.2
  15.8 0.0 copy-start.3
  15.8 1.2 copy-done.3
  17.0 2.1 %split_heads.1 = bf16[32,256,128]{2,1,0:T(8,128)(2,1)} custom-call(bf16[128,4096]{1,0:T(8,128)(2,1)S(1)} %copy-done.2, bf16[128,4096]{1,0:T(8,128)(2,1)S(1)} %copy-done.3), custom_call_target="tpu_custom_call" | custom-call | tf_op jit(solution)/shard_map/split_heads/pallas_call | solution.py:71
  19.1 2.6 %all-to-all-done.3.rows_ref = bf16[32,8,128]{2,1,0:T(8,128)(2,1)S(1)} async-done(((bf16[32,8,128]{2,1,0:T(8,128)(2,1)}), bf16[32,8,128]{2,1,0:T(8,128)(2,1)S(1)}, u32[]{:S(2)}, u32[]{:S(2)}) %all-to-all-start.3) | async-done | bytes 65568 | tf_op jit(solution)/shard_map/all_to_all | solution.py:305
  21.6 4.8 %all-to-all-start.4 = ((bf16[32,256,128]{2,1,0:T(8,128)(2,1)}), bf16[32,256,128]{2,1,0:T(8,128)(2,1)S(1)}, u32[]{:S(2)}, u32[]{:S(2)}) async-start(bf16[32,256,128]{2,1,0:T(8,128)(2,1)} %split_heads.1), calls=%async_computation.4 | async-start | bytes 4194304 | tf_op jit(solution)/shard_map/all_to_all | solution.py:305
  27.1 0.6 compact.1
  27.7 33.9 %all-gather = bf16[3328,128]{1,0:T(8,128)(2,1)S(1)} all-gather(bf16[208,128]{1,0:T(8,128)(2,1)S(1)} %get-tuple-element.57), channel_id=2, replica_groups=mesh['zo'=8,'zi'=2,'c'=2,'blk'=16] {'zo','zi'}, dimensions={0}, use_global_device_ids=true | all-gather | bytes 905216 | tf_op jit(solution)/shard_map/all_gather | solution.py:324
  61.5 0.0 copy-start.5
  61.6 0.9 copy-done.5
  62.5 0.6 slice_reduce_fusion
  64.4 0.0 all-to-all-done.4
  64.4 39.3 %conditional.1 = (bf16[32,8,128]{2,1,0:T(8,128)(2,1)}) conditional(s32[]{:T(128)} %clamp.3, (s32[1]{0:T(128)}, bf16[8,2,208,128]{3,2,1,0:T(8,128)(2,1)}, bf16[32,256,128]{2,1,0:T(8,128)(2,1)S(1)}, bf16[208,128]{1,0:T(8,128)(2,1)S(1)}, bf16[256,256]{1,0:T(8,128)(2,1)S(1)}) %tuple.20, (s32[1]{0:T(128)}, ...), branch_computations={%region_1.0_spmd, %region_2.0_spmd, %region_3.0_spmd} | conditional | flops 12884901888 | bytes 18546776 | solution.py:328
  64.4 0.0 copy-start.6
  64.4 6.7 %attend.7 = bf16[8,144,128]{2,1,0:T(8,128)(2,1)S(1)} custom-call(s32[1]{0:T(128)S(6)} %sub.6.side_ref, bf16[8,2,208,128]{3,2,1,0:T(8,128)(2,1)} %get-tuple-element.40.query_ref, bf16[32,256,128]{2,1,0:T(8,128)(2,1)S(1)} %get-tuple-element.41.kv_ref), custom_call_target="tpu_custom_call" | custom-call | flops 4294967296 | bytes 6291456 | tf_op jit(solution)/shard_map/cond/branch_0_fun/attend/pallas_call | solution.py:204
  71.2 2.1 %collective-permute-start = (bf16[8,144,128]{2,1,0:T(8,128)(2,1)S(1)}, bf16[8,144,128]{2,1,0:T(8,128)(2,1)S(1)}, u32[]{:S(2)}, u32[]{:S(2)}) collective-permute-start(bf16[8,144,128]{2,1,0:T(8,128)(2,1)S(1)} %attend.7), channel_id=1, source_target_pairs={{0,32},{32,0},{1,33},{33,1},{2,34},{34,2},{3,35},{35,3},{4,36},{36... | collective-permute-start | bytes 884744 | tf_op jit(solution)/shard_map/cond/branch_0_fun/ppermute | solution.py:310
  73.3 0.0 copy-done.6
  73.3 5.7 %attend.6.own_ref = bf16[8,144,128]{2,1,0:T(8,128)(2,1)S(1)} custom-call(s32[1]{0:T(128)} %get-tuple-element.38.side_ref, bf16[8,2,208,128]{3,2,1,0:T(8,128)(2,1)S(1)} %copy-done.6, bf16[32,256,128]{2,1,0:T(8,128)(2,1)S(1)} %get-tuple-element.41.kv_ref), custom_call_target="tpu_custom_call" | custom-call | flops 4294967296 | bytes 6291456 | tf_op jit(solution)/shard_map/cond/branch_0_fun/attend/pallas_call | solution.py:204
  79.0 0.0 collective-permute-done.other_ref
  79.0 0.5 merge_pair.3
  79.5 23.2 %all_to_all.27.parts_ref = bf16[8,144,128]{2,1,0:T(8,128)(2,1)S(1)} all-to-all(bf16[8,144,128]{2,1,0:T(8,128)(2,1)S(1)} %merge_pair.3), channel_id=1, replica_groups=mesh['zo'=8,'zi'=2,'c'=2,'blk'=16] {'zo'}, dimensions={0} | all-to-all | bytes 589824 | tf_op jit(solution)/shard_map/cond/branch_0_fun/all_to_all | solution.py:305
  102.7 1.0 finish.3
  103.7 14.1 %all-to-all-start.5 = ((bf16[32,8,128]{2,1,0:T(8,128)(2,1)}), bf16[32,8,128]{2,1,0:T(8,128)(2,1)S(1)}, u32[]{:S(2)}, u32[]{:S(2)}) async-start(bf16[32,8,128]{2,1,0:T(8,128)(2,1)} %get-tuple-element.60), calls=%async_computation.5 | async-start | bytes 131072 | tf_op jit(solution)/shard_map/all_to_all | solution.py:305
  117.9 0.0 copy-done
  117.9 7.1 %all-to-all-done.5.rows_ref = bf16[32,8,128]{2,1,0:T(8,128)(2,1)S(1)} async-done(((bf16[32,8,128]{2,1,0:T(8,128)(2,1)}), bf16[32,8,128]{2,1,0:T(8,128)(2,1)S(1)}, u32[]{:S(2)}, u32[]{:S(2)}) %all-to-all-start.5) | async-done | bytes 65568 | tf_op jit(solution)/shard_map/all_to_all | solution.py:305
  125.0 0.6 apply_gate.1
  (1 shorter events, 0.0 us)
Async XLA Ops:
  0.0 117.9 %copy-start = (f32[50,4096]{1,0:T(8,128)S(1)}, f32[50,4096]{1,0:T(8,128)}, u32[]{:S(2)}) copy-start(f32[50,4096]{1,0:T(8,128)} %param.16) | copy-start | bytes 2457604
  0.7 1.2 copy-start.1
  2.0 0.7 copy-start.4
  4.0 17.6 %all-to-all-start.3 = ((bf16[32,8,128]{2,1,0:T(8,128)(2,1)}), bf16[32,8,128]{2,1,0:T(8,128)(2,1)S(1)}, u32[]{:S(2)}, u32[]{:S(2)}) async-start(bf16[32,8,128]{2,1,0:T(8,128)(2,1)} %choose.1), calls=%async_computation.3 | async-start | bytes 131072 | tf_op jit(solution)/shard_map/all_to_all | solution.py:305
  14.5 1.2 copy-start.2
  15.8 1.2 copy-start.3
  21.6 42.7 %all-to-all-start.4 = ((bf16[32,256,128]{2,1,0:T(8,128)(2,1)}), bf16[32,256,128]{2,1,0:T(8,128)(2,1)S(1)}, u32[]{:S(2)}, u32[]{:S(2)}) async-start(bf16[32,256,128]{2,1,0:T(8,128)(2,1)} %split_heads.1), calls=%async_computation.4 | async-start | bytes 4194304 | tf_op jit(solution)/shard_map/all_to_all | solution.py:305
  61.5 0.9 copy-start.5
  64.4 8.9 %copy-start.6 = (bf16[8,2,208,128]{3,2,1,0:T(8,128)(2,1)S(1)}, bf16[8,2,208,128]{3,2,1,0:T(8,128)(2,1)}, u32[]{:S(2)}) copy-start(bf16[8,2,208,128]{3,2,1,0:T(8,128)(2,1)} %get-tuple-element.40.query_ref) | copy-start | bytes 2555908 | tf_op jit(solution)/shard_map/cond
  71.2 7.8 %collective-permute-start = (bf16[8,144,128]{2,1,0:T(8,128)(2,1)S(1)}, bf16[8,144,128]{2,1,0:T(8,128)(2,1)S(1)}, u32[]{:S(2)}, u32[]{:S(2)}) collective-permute-start(bf16[8,144,128]{2,1,0:T(8,128)(2,1)S(1)} %attend.7), channel_id=1, source_target_pairs={{0,32},{32,0},{1,33},{33,1},{2,34},{34,2},{3,35},{35,3},{4,36},{36... | collective-permute-start | bytes 884744 | tf_op jit(solution)/shard_map/cond/branch_0_fun/ppermute | solution.py:310
  103.7 21.3 %all-to-all-start.5 = ((bf16[32,8,128]{2,1,0:T(8,128)(2,1)}), bf16[32,8,128]{2,1,0:T(8,128)(2,1)S(1)}, u32[]{:S(2)}, u32[]{:S(2)}) async-start(bf16[32,8,128]{2,1,0:T(8,128)(2,1)} %get-tuple-element.60), calls=%async_computation.5 | async-start | bytes 131072 | tf_op jit(solution)/shard_map/all_to_all | solution.py:305

commit v3 on v2

--- a/solution.py
+++ b/solution.py
@@ -17,8 +17,9 @@
 NZO = 8
 ROWS = HEADS * SLOTS
 TAIL = 16
-MSG = ROWS + TAIL
 TIERS = (128, 144, ROWS)
+FIRST = TIERS[1]
+DEAD = 64.0
 SCALE = math.log2(math.e) / math.sqrt(HD)
 KEYS = HEADS * TOK
 CHUNK = 1024
@@ -55,7 +56,6 @@
         out_shape=jax.ShapeDtypeStruct((HEADS, PAD, HD), BF),
         in_specs=[SMEM, SMEM, VMEM],
         out_specs=VMEM,
-        compiler_params=SMALL,
         name="choose",
     )(index, counts, query)
 
@@ -74,7 +74,6 @@
         in_specs=[pl.BlockSpec((TOK, per * HD), lambda i: (0, i))] * 2,
         out_specs=pl.BlockSpec((per, 2 * TOK, HD), lambda i: (i, 0, 0)),
         out_shape=jax.ShapeDtypeStruct((HEADS, 2 * TOK, HD), BF),
-        compiler_params=SMALL,
         name="split_heads",
     )(key, value)
 
@@ -101,16 +100,16 @@
     live_row = jnp.broadcast_to(live_row[:1], (n, n))
     move = jnp.where(pos_row == down.astype(F32), live_row, 0.0).astype(BF)
     moved = jnp.dot(move, rows, preferred_element_type=F32)
-    out_ref[:ROWS] = moved[:ROWS].astype(BF)
     total = jnp.sum(live_col, axis=0, keepdims=True)
-    out_ref[ROWS:] = jnp.broadcast_to(total, (TAIL, HD)).astype(BF)
+    alive = iota((ROWS, HD), 0).astype(F32) < total
+    out_ref[...] = jnp.where(alive, moved[:ROWS], DEAD).astype(BF)
 
 
 def compact(rows):
     n = HEADS * PAD
     return pl.pallas_call(
         compact_body,
-        out_shape=(jax.ShapeDtypeStruct((MSG, HD), BF), jax.ShapeDtypeStruct((n, n), BF)),
+        out_shape=(jax.ShapeDtypeStruct((ROWS, HD), BF), jax.ShapeDtypeStruct((n, n), BF)),
         in_specs=[VMEM],
         out_specs=(VMEM, VMEM),
         compiler_params=SMALL,
@@ -160,12 +159,14 @@
     return jnp.concatenate(out, 0)
 
 
-def attend_rows(group, rows, query_ref, kv_ref, out_ref):
-    size = group * rows
-    query = query_ref[:, 0, :rows, :].reshape(size, HD)
+def attend_rows(rows, side, query_ref, kv_ref, out_ref, copies=()):
+    size = NZO * rows
+    query = query_ref[:, side, :rows, :].reshape(size, HD)
     per = CHUNK // TOK
     top = mixed = total = None
     for j in range(KEYS // CHUNK):
+        if j < len(copies):
+            copies[j].wait()
         keys = kv_ref[j * per:(j + 1) * per, :TOK, :].reshape(CHUNK, HD)
         values = kv_ref[j * per:(j + 1) * per, TOK:, :].reshape(CHUNK, HD)
         scores = lax.dot_general(query, keys, NT, preferred_element_type=F32)
@@ -188,36 +189,60 @@
             total = total * fade + part_total
         top = peak
     total = jnp.sum(total, axis=1, keepdims=True)
-    out_ref[:, :rows, :] = (mixed / total).astype(BF).reshape(group, rows, HD)
+    out_ref[:, :rows, :] = (mixed / total).astype(BF).reshape(NZO, rows, HD)
     level = top[:, :1] + jnp.log2(total)
-    for g in range(group):
+    for g in range(NZO):
         out_ref[g, rows:, :] = tail_of(*column_to_lanes(level[g * rows:(g + 1) * rows]))
 
 
-def attend_body(group, rows, side_ref, query_ref, kv_ref, out_ref):
-    attend_rows(group, rows, query_ref, kv_ref, out_ref)
+def load_and_attend_body(rows, side_ref, query_ref, far_ref, out_ref, kv_ref, sems):
+    per = CHUNK // TOK
+    copies = []
+    for i, (at, size) in enumerate(((0, per), (per, HEADS - per))):
+        here = pl.ds(at, size)
+        copies.append(pltpu.make_async_copy(far_ref.at[here], kv_ref.at[here], sems.at[i]))
+        copies[-1].start()
+    attend_rows(rows, side_ref[0], query_ref, kv_ref, out_ref, copies)
+
+
+def attend_body(rows, side_ref, query_ref, kv_ref, out_ref):
+    attend_rows(rows, side_ref[0], query_ref, kv_ref, out_ref)
+
+
+def attend_options(rows):
+    return dict(
+        compiler_params=pltpu.CompilerParams(vmem_limit_bytes=32 * 2**20),
+        cost_estimate=pl.CostEstimate(
+            flops=NZO * rows * KEYS * HD * 8,
+            bytes_accessed=6 * 2**20,
+            transcendentals=NZO * rows * KEYS,
+        ),
+    )
+
+
+def load_and_attend(rows, side, query, kv):
+    return pl.pallas_call(
+        functools.partial(load_and_attend_body, rows),
+        out_shape=(
+            jax.ShapeDtypeStruct((NZO, rows + TAIL, HD), BF),
+            jax.ShapeDtypeStruct(kv.shape, BF),
+        ),
+        in_specs=[SMEM, VMEM, pl.BlockSpec(memory_space=pl.ANY)],
+        out_specs=(VMEM, VMEM),
+        scratch_shapes=[pltpu.SemaphoreType.DMA((2,))],
+        name="load_and_attend",
+        **attend_options(rows),
+    )(side, query, kv)
 
 
 def attend(rows, side, query, kv):
-    group = 8 if rows == TIERS[0] else 4
-    work = NZO * rows * KEYS * HD * 4
-    return pl.pallas_call(
-        functools.partial(attend_body, group, rows),
-        grid_spec=pltpu.PrefetchScalarGridSpec(
-            num_scalar_prefetch=1,
-            grid=(NZO // group,),
-            in_specs=[
-                pl.BlockSpec((group, 1, MSG, HD), lambda i, side: (i, side[0], 0, 0)),
-                pl.BlockSpec((HEADS, 2 * TOK, HD), lambda i, side: (0, 0, 0)),
-            ],
-            out_specs=pl.BlockSpec((group, rows + TAIL, HD), lambda i, side: (i, 0, 0)),
-        ),
+    return pl.pallas_call(
+        functools.partial(attend_body, rows),
         out_shape=jax.ShapeDtypeStruct((NZO, rows + TAIL, HD), BF),
-        compiler_params=pltpu.CompilerParams(vmem_limit_bytes=40 * 2**20),
-        cost_estimate=pl.CostEstimate(
-            flops=2 * work, bytes_accessed=6 * 2**20, transcendentals=NZO * rows * KEYS
-        ),
+        in_specs=[SMEM, VMEM, VMEM],
+        out_specs=VMEM,
         name="attend",
+        **attend_options(rows),
     )(side, query, kv)
 
 
@@ -260,8 +285,7 @@
         column = lanes_to_column(weights[i] / both, rows)
         part = parts_ref[i, :rows, :].astype(F32) * column
         mixed = part if mixed is None else mixed + part
-    count = live_ref[ROWS:, :].astype(F32)[:1]
-    alive = iota((rows, HD), 0).astype(F32) < count
+    alive = live_ref[:rows, :].astype(F32) < DEAD / 2
     mixed = jnp.where(alive, mixed, 0.0).astype(BF)
     placed = jnp.dot(back_ref[:, :rows], mixed, preferred_element_type=F32)
     out_ref[...] = placed.reshape(HEADS, PAD, HD).astype(BF)
@@ -305,8 +329,14 @@
     return lax.all_to_all(x, axes, split_axis=0, concat_axis=0, tiled=True)
 
 
+def gather_z(x):
+    return lax.all_gather(x, ("zo", "zi"), axis=0, tiled=False).reshape(NZO, 2, -1, HD)
+
+
 def late(size, side, rows, kv, live, back):
-    away = attend(size, 1 - side, rows, kv)
+    if size > FIRST:
+        rows = jnp.concatenate([rows, gather_z(live[FIRST:])], axis=2)
+    away, kv = load_and_attend(size, 1 - side, rows, kv)
     arrived = lax.ppermute(away, "zi", [(0, 1), (1, 0)])
     own = attend(size, side, rows, kv)
     merged = merge_pair(own, arrived)
@@ -321,10 +351,10 @@
     plane_rows = swap(mine, PLANE)
     kv = swap(after(kv, plane_rows), PLANE)
     live, back = compact(plane_rows)
-    rows = lax.all_gather(live, ("zo", "zi"), axis=0, tiled=False)
-    rows = rows.reshape(NZO, 2, MSG, HD)
-    most = jnp.max(rows[:, :, ROWS, 0].astype(F32))
-    tier = sum((most > limit).astype(jnp.int32) for limit in TIERS[:-1])
+    rows = gather_z(live[:FIRST])
+    tail = rows[:, :, TIERS[0]:, 0]
+    fullest = jnp.where(iota(tail.shape, 2) == FIRST - TIERS[0] - 1, 2, 1)
+    tier = jnp.max(jnp.where(tail.astype(F32) < DEAD / 2, fullest, 0))
     sent = lax.switch(tier, [functools.partial(late, n) for n in TIERS], side, rows, kv, live, back)
     heads = swap(sent, PLANE)
     gate = lax.dynamic_slice_in_dim(gate_table, timestep[0], 1, 0)

time: 126 us -> 124 us (0.984)
  local copies, waits for them, and re-layouts: 5.25 us -> 0.2 us
  Pallas kernels: 18.7 us -> 22.6 us
    unnamed x12 -> x3, local copies, waits for them, and re-layouts: 5.23 us -> 0.17 us
    pallas_call x1, Pallas kernels: 2.09 us -> 3.9 us  [split_heads(): pl.pallas_call(functools.partial(split_body, per), grid=(HEADS // per,),...]
    pallas_call x3, Pallas kernels: 13 us -> 14.4 us  [the longest x1 8.15 us: load_and_attend(): pl.pallas_call(functools.partial(load_and_attend_body, rows), out_shape=(...]
  transfers between devices with their start and end apart: 4 -> 4, of which waited for: 2 -> 2; matrix products, arithmetic and copies ran while one was open for 1% -> 1% of each run, Pallas kernels for 7% -> 8%
where the time goes in v3:
time: 124 us
  blocking collectives  56.7 us (46%)
  starting transfers between devices  31.2 us (25%)
  Pallas kernels  22.6 us (18%)
  waiting for transfers between devices  10.3 us (8%)
  between operations  2.12 us (2%)
    all_gather x1, blocking collectives, gather_z(): lax.all_gather(x, ('zo', 'zi'), axis=0, tiled=False).reshape(NZO, 2, -1, HD)  32.8 us
    all_to_all x3, starting transfers between devices, swap(): return lax.all_to_all(x, axes, split_axis=0, concat_axis=0, tiled=True)  29.1 us
    all_to_all x1, blocking collectives, swap(): return lax.all_to_all(x, axes, split_axis=0, concat_axis=0, tiled=True)  23.9 us
    all_to_all x3, waiting for transfers between devices, swap(): return lax.all_to_all(x, axes, split_axis=0, concat_axis=0, tiled=True)  10.3 us
    pallas_call x1, Pallas kernels, load_and_attend(): pl.pallas_call(functools.partial(load_and_attend_body, rows), out_shape=(...  8.15 us
    pallas_call x1, Pallas kernels, attend(): pl.pallas_call(functools.partial(attend_body, rows), out_shape=jax.ShapeD...  5.67 us
    pallas_call x1, Pallas kernels, split_heads(): pl.pallas_call(functools.partial(split_body, per), grid=(HEADS // per,),...  3.9 us
  transfers between devices with their start and end apart: 4, of which 2 were waited for; matrix products, arithmetic and copies ran while one was open for 1% of the time, Pallas kernels for 8%

profile of v3, /device:TPU:1, one launch (start us, length us, event | category | flops | bytes accessed | tf_op | source)
XLA Modules:
  0.0 123.8 jit_solution(3135364819514730759)
XLA Ops:
  0.0 0.0 copy-start
  0.7 2.1 %choose.1 = bf16[32,8,128]{2,1,0:T(8,128)(2,1)} custom-call(s32[6]{0:T(128)} %index_ref.1, s32[1]{0:T(128)S(6)} %copy.13.count_ref, bf16[128,4096]{1,0:T(8,128)(2,1)} %query_ref.1), custom_call_target="tpu_custom_call" | custom-call | tf_op jit(solution)/shard_map/choose/pallas_call | solution.py:54
  2.9 10.5 %all-to-all-start.3 = ((bf16[32,8,128]{2,1,0:T(8,128)(2,1)}), bf16[32,8,128]{2,1,0:T(8,128)(2,1)S(1)}, u32[]{:S(2)}, u32[]{:S(2)}) async-start(bf16[32,8,128]{2,1,0:T(8,128)(2,1)} %choose.1), calls=%async_computation.3 | async-start | bytes 131072 | tf_op jit(solution)/shard_map/all_to_all | solution.py:329
  13.3 3.9 %split_heads.1 = bf16[32,256,128]{2,1,0:T(8,128)(2,1)} custom-call(bf16[128,4096]{1,0:T(8,128)(2,1)} %key_ref.1, bf16[128,4096]{1,0:T(8,128)(2,1)} %value_ref.1), custom_call_target="tpu_custom_call" | custom-call | tf_op jit(solution)/shard_map/split_heads/pallas_call | solution.py:71
  17.2 3.2 %all-to-all-done.3.rows_ref = bf16[32,8,128]{2,1,0:T(8,128)(2,1)S(1)} async-done(((bf16[32,8,128]{2,1,0:T(8,128)(2,1)}), bf16[32,8,128]{2,1,0:T(8,128)(2,1)S(1)}, u32[]{:S(2)}, u32[]{:S(2)}) %all-to-all-start.3) | async-done | bytes 65568 | tf_op jit(solution)/shard_map/all_to_all | solution.py:329
  20.5 5.0 %all-to-all-start.4 = ((bf16[32,256,128]{2,1,0:T(8,128)(2,1)}), bf16[32,256,128]{2,1,0:T(8,128)(2,1)}, u32[]{:S(2)}, u32[]{:S(2)}) async-start(bf16[32,256,128]{2,1,0:T(8,128)(2,1)} %split_heads.1), calls=%async_computation.4 | async-start | bytes 4194304 | tf_op jit(solution)/shard_map/all_to_all | solution.py:329
  26.1 0.6 compact.1
  26.7 32.8 %all-gather.1 = bf16[2304,128]{1,0:T(8,128)(2,1)S(1)} all-gather(bf16[144,128]{1,0:T(8,128)(2,1)S(1)} %slice.9), channel_id=3, replica_groups=mesh['zo'=8,'zi'=2,'c'=2,'blk'=16] {'zo','zi'}, dimensions={0}, use_global_device_ids=true | all-gather | bytes 626688 | tf_op jit(solution)/shard_map/all_gather | solution.py:333
  59.5 0.2 copy.9
  59.7 0.7 select_reduce_fusion
  61.0 0.0 all-to-all-done.4
  61.0 41.4 %conditional.1 = (bf16[32,8,128]{2,1,0:T(8,128)(2,1)}) conditional(s32[]{:T(128)} %clamp.3, (s32[1]{0:T(128)}, bf16[8,2,144,128]{3,2,1,0:T(8,128)(2,1)S(1)}, bf16[32,256,128]{2,1,0:T(8,128)(2,1)}, bf16[192,128]{1,0:T(8,128)(2,1)S(1)}, bf16[256,256]{1,0:T(8,128)(2,1)S(1)}) %tuple.21, (s32[1]{0:T(128)}, ...), branch_computations={%region_1.2_spmd, %region_2.3_spmd, %region_3.4_spmd} | conditional | flops 12886474752 | bytes 16945212 | solution.py:358
  61.0 8.1 %load_and_attend.3 = (bf16[8,144,128]{2,1,0:T(8,128)(2,1)S(1)}, bf16[32,256,128]{2,1,0:T(8,128)(2,1)S(1)}) custom-call(s32[1]{0:T(128)S(6)} %sub.6.side_ref, bf16[8,2,144,128]{3,2,1,0:T(8,128)(2,1)S(1)} %get-tuple-element.40.query_ref, bf16[32,256,128]{2,1,0:T(8,128)(2,1)} %get-tuple-element.41.far_ref), custom_call_target="tpu_custom_call" | custom-call | flops 4294967296 | bytes 6291456 | tf_op jit(solution)/shard_map/cond/branch_0_fun/load_and_attend/pallas_call | solution.py:224
  69.2 2.1 %collective-permute-start = (bf16[8,144,128]{2,1,0:T(8,128)(2,1)S(1)}, bf16[8,144,128]{2,1,0:T(8,128)(2,1)S(1)}, u32[]{:S(2)}, u32[]{:S(2)}) collective-permute-start(bf16[8,144,128]{2,1,0:T(8,128)(2,1)S(1)} %get-tuple-element.43), channel_id=1, source_target_pairs={{0,32},{32,0},{1,33},{33,1},{2,34},{34,2},{3,35},{35,3},{4,36},{36... | collective-permute-start | bytes 884744 | tf_op jit(solution)/shard_map/cond/branch_0_fun/ppermute | solution.py:340
  71.3 5.7 %attend.3.own_ref = bf16[8,144,128]{2,1,0:T(8,128)(2,1)S(1)} custom-call(s32[1]{0:T(128)} %get-tuple-element.38.side_ref, bf16[8,2,144,128]{3,2,1,0:T(8,128)(2,1)S(1)} %get-tuple-element.40.query_ref, bf16[32,256,128]{2,1,0:T(8,128)(2,1)S(1)} %get-tuple-element.42.kv_ref), custom_call_target="tpu_custom_call" | custom-call | flops 4294967296 | bytes 6291456 | tf_op jit(solution)/shard_map/cond/branch_0_fun/attend/pallas_call | solution.py:239
  76.9 0.0 collective-permute-done.other_ref
  77.0 0.5 merge_pair.3
  77.5 23.9 %all_to_all.27.parts_ref = bf16[8,144,128]{2,1,0:T(8,128)(2,1)S(1)} all-to-all(bf16[8,144,128]{2,1,0:T(8,128)(2,1)S(1)} %merge_pair.3), channel_id=1, replica_groups=mesh['zo'=8,'zi'=2,'c'=2,'blk'=16] {'zo'}, dimensions={0} | all-to-all | bytes 589824 | tf_op jit(solution)/shard_map/cond/branch_0_fun/all_to_all | solution.py:329
  101.4 1.0 finish.3
  102.4 13.6 %all-to-all-start.5 = ((bf16[32,8,128]{2,1,0:T(8,128)(2,1)}), bf16[32,8,128]{2,1,0:T(8,128)(2,1)S(1)}, u32[]{:S(2)}, u32[]{:S(2)}) async-start(bf16[32,8,128]{2,1,0:T(8,128)(2,1)} %get-tuple-element.66), calls=%async_computation.5 | async-start | bytes 131072 | tf_op jit(solution)/shard_map/all_to_all | solution.py:329
  116.0 0.0 copy-done
  116.0 7.1 %all-to-all-done.5.rows_ref = bf16[32,8,128]{2,1,0:T(8,128)(2,1)S(1)} async-done(((bf16[32,8,128]{2,1,0:T(8,128)(2,1)}), bf16[32,8,128]{2,1,0:T(8,128)(2,1)S(1)}, u32[]{:S(2)}, u32[]{:S(2)}) %all-to-all-start.5) | async-done | bytes 65568 | tf_op jit(solution)/shard_map/all_to_all | solution.py:329
  123.1 0.6 apply_gate.1
  (4 shorter events, 0.0 us)
Async XLA Ops:
  0.0 116.0 %copy-start = (f32[50,4096]{1,0:T(8,128)S(1)}, f32[50,4096]{1,0:T(8,128)}, u32[]{:S(2)}) copy-start(f32[50,4096]{1,0:T(8,128)} %param.16) | copy-start | bytes 2457604
  2.9 17.6 %all-to-all-start.3 = ((bf16[32,8,128]{2,1,0:T(8,128)(2,1)}), bf16[32,8,128]{2,1,0:T(8,128)(2,1)S(1)}, u32[]{:S(2)}, u32[]{:S(2)}) async-start(bf16[32,8,128]{2,1,0:T(8,128)(2,1)} %choose.1), calls=%async_computation.3 | async-start | bytes 131072 | tf_op jit(solution)/shard_map/all_to_all | solution.py:329
  20.5 40.5 %all-to-all-start.4 = ((bf16[32,256,128]{2,1,0:T(8,128)(2,1)}), bf16[32,256,128]{2,1,0:T(8,128)(2,1)}, u32[]{:S(2)}, u32[]{:S(2)}) async-start(bf16[32,256,128]{2,1,0:T(8,128)(2,1)} %split_heads.1), calls=%async_computation.4 | async-start | bytes 4194304 | tf_op jit(solution)/shard_map/all_to_all | solution.py:329
  69.2 7.8 %collective-permute-start = (bf16[8,144,128]{2,1,0:T(8,128)(2,1)S(1)}, bf16[8,144,128]{2,1,0:T(8,128)(2,1)S(1)}, u32[]{:S(2)}, u32[]{:S(2)}) collective-permute-start(bf16[8,144,128]{2,1,0:T(8,128)(2,1)S(1)} %get-tuple-element.43), channel_id=1, source_target_pairs={{0,32},{32,0},{1,33},{33,1},{2,34},{34,2},{3,35},{35,3},{4,36},{36... | collective-permute-start | bytes 884744 | tf_op jit(solution)/shard_map/cond/branch_0_fun/ppermute | solution.py:340
  102.4 20.8 %all-to-all-start.5 = ((bf16[32,8,128]{2,1,0:T(8,128)(2,1)}), bf16[32,8,128]{2,1,0:T(8,128)(2,1)S(1)}, u32[]{:S(2)}, u32[]{:S(2)}) async-start(bf16[32,8,128]{2,1,0:T(8,128)(2,1)} %get-tuple-element.66), calls=%async_computation.5 | async-start | bytes 131072 | tf_op jit(solution)/shard_map/all_to_all | solution.py:329

commit v4 on v2

--- a/solution.py
+++ b/solution.py
@@ -17,8 +17,8 @@
 NZO = 8
 ROWS = HEADS * SLOTS
 TAIL = 16
-MSG = ROWS + TAIL
-TIERS = (128, 144, ROWS)
+FIRST = 144
+DEAD = 64.0
 SCALE = math.log2(math.e) / math.sqrt(HD)
 KEYS = HEADS * TOK
 CHUNK = 1024
@@ -55,7 +55,6 @@
         out_shape=jax.ShapeDtypeStruct((HEADS, PAD, HD), BF),
         in_specs=[SMEM, SMEM, VMEM],
         out_specs=VMEM,
-        compiler_params=SMALL,
         name="choose",
     )(index, counts, query)
 
@@ -74,12 +73,11 @@
         in_specs=[pl.BlockSpec((TOK, per * HD), lambda i: (0, i))] * 2,
         out_specs=pl.BlockSpec((per, 2 * TOK, HD), lambda i: (i, 0, 0)),
         out_shape=jax.ShapeDtypeStruct((HEADS, 2 * TOK, HD), BF),
-        compiler_params=SMALL,
         name="split_heads",
     )(key, value)
 
 
-def compact_body(rows_ref, out_ref, back_ref):
+def compact_body(kept, rows_ref, out_ref, back_ref):
     n = HEADS * PAD
     rows = rows_ref[...].astype(F32).reshape(n, HD).astype(BF)
     down, across = iota((n, n), 0), iota((n, n), 1)
@@ -101,16 +99,16 @@
     live_row = jnp.broadcast_to(live_row[:1], (n, n))
     move = jnp.where(pos_row == down.astype(F32), live_row, 0.0).astype(BF)
     moved = jnp.dot(move, rows, preferred_element_type=F32)
-    out_ref[:ROWS] = moved[:ROWS].astype(BF)
     total = jnp.sum(live_col, axis=0, keepdims=True)
-    out_ref[ROWS:] = jnp.broadcast_to(total, (TAIL, HD)).astype(BF)
-
-
-def compact(rows):
+    alive = iota((kept, HD), 0).astype(F32) < total
+    out_ref[...] = jnp.where(alive, moved[:kept], DEAD).astype(BF)
+
+
+def compact(kept, rows):
     n = HEADS * PAD
     return pl.pallas_call(
-        compact_body,
-        out_shape=(jax.ShapeDtypeStruct((MSG, HD), BF), jax.ShapeDtypeStruct((n, n), BF)),
+        functools.partial(compact_body, kept),
+        out_shape=(jax.ShapeDtypeStruct((kept, HD), BF), jax.ShapeDtypeStruct((n, n), BF)),
         in_specs=[VMEM],
         out_specs=(VMEM, VMEM),
         compiler_params=SMALL,
@@ -160,9 +158,10 @@
     return jnp.concatenate(out, 0)
 
 
-def attend_rows(group, rows, query_ref, kv_ref, out_ref):
-    size = group * rows
-    query = query_ref[:, 0, :rows, :].reshape(size, HD)
+def attend_body(side_ref, query_ref, kv_ref, out_ref):
+    rows = query_ref.shape[2]
+    size = NZO * rows
+    query = query_ref[:, side_ref[0], :, :].reshape(size, HD)
     per = CHUNK // TOK
     top = mixed = total = None
     for j in range(KEYS // CHUNK):
@@ -188,34 +187,24 @@
             total = total * fade + part_total
         top = peak
     total = jnp.sum(total, axis=1, keepdims=True)
-    out_ref[:, :rows, :] = (mixed / total).astype(BF).reshape(group, rows, HD)
+    out_ref[:, :rows, :] = (mixed / total).astype(BF).reshape(NZO, rows, HD)
     level = top[:, :1] + jnp.log2(total)
-    for g in range(group):
+    for g in range(NZO):
         out_ref[g, rows:, :] = tail_of(*column_to_lanes(level[g * rows:(g + 1) * rows]))
 
 
-def attend_body(group, rows, side_ref, query_ref, kv_ref, out_ref):
-    attend_rows(group, rows, query_ref, kv_ref, out_ref)
-
-
-def attend(rows, side, query, kv):
-    group = 8 if rows == TIERS[0] else 4
-    work = NZO * rows * KEYS * HD * 4
-    return pl.pallas_call(
-        functools.partial(attend_body, group, rows),
-        grid_spec=pltpu.PrefetchScalarGridSpec(
-            num_scalar_prefetch=1,
-            grid=(NZO // group,),
-            in_specs=[
-                pl.BlockSpec((group, 1, MSG, HD), lambda i, side: (i, side[0], 0, 0)),
-                pl.BlockSpec((HEADS, 2 * TOK, HD), lambda i, side: (0, 0, 0)),
-            ],
-            out_specs=pl.BlockSpec((group, rows + TAIL, HD), lambda i, side: (i, 0, 0)),
-        ),
+def attend(side, query, kv):
+    rows = query.shape[2]
+    return pl.pallas_call(
+        attend_body,
         out_shape=jax.ShapeDtypeStruct((NZO, rows + TAIL, HD), BF),
-        compiler_params=pltpu.CompilerParams(vmem_limit_bytes=40 * 2**20),
+        in_specs=[SMEM, VMEM, VMEM],
+        out_specs=VMEM,
+        compiler_params=pltpu.CompilerParams(vmem_limit_bytes=32 * 2**20),
         cost_estimate=pl.CostEstimate(
-            flops=2 * work, bytes_accessed=6 * 2**20, transcendentals=NZO * rows * KEYS
+            flops=NZO * rows * KEYS * HD * 8,
+            bytes_accessed=6 * 2**20,
+            transcendentals=NZO * rows * KEYS,
         ),
         name="attend",
     )(side, query, kv)
@@ -260,8 +249,7 @@
         column = lanes_to_column(weights[i] / both, rows)
         part = parts_ref[i, :rows, :].astype(F32) * column
         mixed = part if mixed is None else mixed + part
-    count = live_ref[ROWS:, :].astype(F32)[:1]
-    alive = iota((rows, HD), 0).astype(F32) < count
+    alive = live_ref[...].astype(F32) < DEAD / 2
     mixed = jnp.where(alive, mixed, 0.0).astype(BF)
     placed = jnp.dot(back_ref[:, :rows], mixed, preferred_element_type=F32)
     out_ref[...] = placed.reshape(HEADS, PAD, HD).astype(BF)
@@ -305,30 +293,36 @@
     return lax.all_to_all(x, axes, split_axis=0, concat_axis=0, tiled=True)
 
 
-def late(size, side, rows, kv, live, back):
-    away = attend(size, 1 - side, rows, kv)
-    arrived = lax.ppermute(away, "zi", [(0, 1), (1, 0)])
-    own = attend(size, side, rows, kv)
-    merged = merge_pair(own, arrived)
-    parts = swap(merged, "zo")
-    return finish(parts, live, back)
-
-
-def local(query, key, value, index, counts, timestep, gate_table):
+def whole(kept, query, key, value, index, counts, gate):
     side = lax.axis_index("zi").astype(jnp.int32).reshape(1)
     mine = choose(query, index, counts)
     kv = split_heads(key, value)
     plane_rows = swap(mine, PLANE)
     kv = swap(after(kv, plane_rows), PLANE)
-    live, back = compact(plane_rows)
-    rows = lax.all_gather(live, ("zo", "zi"), axis=0, tiled=False)
-    rows = rows.reshape(NZO, 2, MSG, HD)
-    most = jnp.max(rows[:, :, ROWS, 0].astype(F32))
-    tier = sum((most > limit).astype(jnp.int32) for limit in TIERS[:-1])
-    sent = lax.switch(tier, [functools.partial(late, n) for n in TIERS], side, rows, kv, live, back)
-    heads = swap(sent, PLANE)
+    live, back = compact(kept, plane_rows)
+    rows = lax.all_gather(live, ("zo", "zi"), axis=0, tiled=False).reshape(NZO, 2, kept, HD)
+    away = attend(1 - side, rows, kv)
+    arrived = lax.ppermute(away, "zi", [(0, 1), (1, 0)])
+    own = attend(side, rows, kv)
+    merged = merge_pair(own, arrived)
+    parts = swap(merged, "zo")
+    heads = swap(finish(parts, live, back), PLANE)
+    return apply_gate(counts, heads, gate), rows
+
+
+def local(query, key, value, index, counts, timestep, gate_table):
     gate = lax.dynamic_slice_in_dim(gate_table, timestep[0], 1, 0)
-    return apply_gate(counts, heads, gate)
+    usual, rows = whole(FIRST, query, key, value, index, counts, gate)
+    full = jnp.min(rows[:, :, FIRST - 1, 0].astype(F32)) < DEAD / 2
+    full, usual = lax.optimization_barrier((full, usual))
+
+    def again(usual, *args):
+        return whole(ROWS, *args)[0]
+
+    def keep(usual, *args):
+        return usual
+
+    return lax.cond(full, again, keep, usual, query, key, value, index, counts, gate)
 
 
 def solution(mesh):

time: 126 us -> 126 us (level)
  blocking collectives: 57.1 us -> 33.1 us
  waiting for transfers between devices: 9.67 us -> 23.7 us
  starting transfers between devices: 31.5 us -> 40.5 us
  Pallas kernels: 18.7 us -> 22.4 us
  local copies, waits for them, and re-layouts: 5.25 us -> 1.73 us
    all_to_all x1 -> x0, blocking collectives: 23.2 us -> none  [swap(): return lax.all_to_all(x, axes, split_axis=0, concat_axis=0, tiled=True)]
    all_to_all x3 -> x4, waiting for transfers between devices: 9.66 us -> 23.7 us  [swap(): return lax.all_to_all(x, axes, split_axis=0, concat_axis=0, tiled=True)]
    all_to_all x3 -> x4, starting transfers between devices: 29.4 us -> 38.4 us  [swap(): return lax.all_to_all(x, axes, split_axis=0, concat_axis=0, tiled=True)]
    unnamed x12, local copies, waits for them, and re-layouts: 5.23 us -> 1.71 us
    pallas_call x1, Pallas kernels: 2.09 us -> 3.91 us  [split_heads(): pl.pallas_call(functools.partial(split_body, per), grid=(HEADS // per,),...]
    reduce_min x0 -> x1, other arithmetic: none -> 1.45 us  [local(): full = jnp.min(rows[:, :, FIRST - 1, 0].astype(F32)) < DEAD / 2]
  transfers between devices with their start and end apart: 4 -> 5, of which waited for: 2 -> 3; matrix products, arithmetic and copies ran while one was open for 1% -> 1% of each run, Pallas kernels for 7% -> 9%
where the time goes in v4:
time: 126 us; the launch traced here: 125 us
  starting transfers between devices  40.5 us (32%)
  blocking collectives  33.1 us (26%)
  waiting for transfers between devices  23.7 us (19%)
  Pallas kernels  22.4 us (18%)
  between operations  2.17 us (2%)
  local copies, waits for them, and re-layouts  1.73 us (1%)
  other arithmetic  1.45 us (1%)
    all_to_all x4, starting transfers between devices, swap(): return lax.all_to_all(x, axes, split_axis=0, concat_axis=0, tiled=True)  38.4 us
    all_gather x1, blocking collectives, whole(): lax.all_gather(live, ('zo', 'zi'), axis=0, tiled=False)  33.1 us
    all_to_all x4, waiting for transfers between devices, swap(): return lax.all_to_all(x, axes, split_axis=0, concat_axis=0, tiled=True)  23.7 us
    pallas_call x2, Pallas kernels, attend(): pl.pallas_call(attend_body, out_shape=jax.ShapeDtypeStruct((NZO, rows + T...  12.9 us
    pallas_call x1, Pallas kernels, split_heads(): pl.pallas_call(functools.partial(split_body, per), grid=(HEADS // per,),...  3.91 us
  transfers between devices with their start and end apart: 5, of which 3 were waited for; matrix products, arithmetic and copies ran while one was open for 1% of the time, Pallas kernels for 9%

profile of v4, /device:TPU:1, one launch (start us, length us, event | category | flops | bytes accessed | tf_op | source)
XLA Modules:
  0.0 125.3 jit_solution(4756883164469806315)
XLA Ops:
  0.0 0.0 copy-start
  0.7 2.1 %choose.3 = bf16[32,8,128]{2,1,0:T(8,128)(2,1)} custom-call(s32[6]{0:T(128)} %index_ref.1, s32[1]{0:T(128)S(6)} %copy.12.count_ref, bf16[128,4096]{1,0:T(8,128)(2,1)} %query_ref.1), custom_call_target="tpu_custom_call" | custom-call | tf_op jit(solution)/shard_map/choose/pallas_call | solution.py:53
  2.9 10.5 %all-to-all-start.4 = ((bf16[32,8,128]{2,1,0:T(8,128)(2,1)}), bf16[32,8,128]{2,1,0:T(8,128)(2,1)S(1)}, u32[]{:S(2)}, u32[]{:S(2)}) async-start(bf16[32,8,128]{2,1,0:T(8,128)(2,1)} %choose.3), calls=%async_computation.4 | async-start | bytes 131072 | tf_op jit(solution)/shard_map/all_to_all | solution.py:293
  13.4 3.9 %split_heads.3 = bf16[32,256,128]{2,1,0:T(8,128)(2,1)} custom-call(bf16[128,4096]{1,0:T(8,128)(2,1)} %key_ref.1, bf16[128,4096]{1,0:T(8,128)(2,1)} %value_ref.1), custom_call_target="tpu_custom_call" | custom-call | tf_op jit(solution)/shard_map/split_heads/pallas_call | solution.py:70
  17.3 3.2 %all-to-all-done.4.rows_ref = bf16[32,8,128]{2,1,0:T(8,128)(2,1)S(1)} async-done(((bf16[32,8,128]{2,1,0:T(8,128)(2,1)}), bf16[32,8,128]{2,1,0:T(8,128)(2,1)S(1)}, u32[]{:S(2)}, u32[]{:S(2)}) %all-to-all-start.4) | async-done | bytes 65568 | tf_op jit(solution)/shard_map/all_to_all | solution.py:293
  20.5 4.3 %all-to-all-start.5 = ((bf16[32,256,128]{2,1,0:T(8,128)(2,1)}), bf16[32,256,128]{2,1,0:T(8,128)(2,1)S(1)}, u32[]{:S(2)}, u32[]{:S(2)}) async-start(bf16[32,256,128]{2,1,0:T(8,128)(2,1)} %split_heads.3), calls=%async_computation.5 | async-start | bytes 4194304 | tf_op jit(solution)/shard_map/all_to_all | solution.py:293
  24.8 0.6 compact.3
  25.4 33.1 %all-gather.1 = bf16[2304,128]{1,0:T(8,128)(2,1)} all-gather(bf16[144,128]{1,0:T(8,128)(2,1)S(1)} %get-tuple-element.35.live_ref), channel_id=3, replica_groups=mesh['zo'=8,'zi'=2,'c'=2,'blk'=16] {'zo','zi'}, dimensions={0}, use_global_device_ids=true | all-gather | bytes 626688 | tf_op jit(solution)/shard_map/all_gather | solution.py:303
  58.5 0.0 all-to-all-done.5.kv_ref
  58.5 0.0 copy-start.3
  58.5 1.1 copy-done.3
  59.6 0.0 copy-start.4
  59.6 6.5 %attend.7 = bf16[8,160,128]{2,1,0:T(8,128)(2,1)S(1)} custom-call(s32[1]{0:T(128)S(6)} %sub.6.side_ref, bf16[8,2,144,128]{3,2,1,0:T(8,128)(2,1)S(1)} %bitcast.11, bf16[32,256,128]{2,1,0:T(8,128)(2,1)S(1)} %all-to-all-done.5.kv_ref), custom_call_target="tpu_custom_call" | custom-call | flops 4831838208 | bytes 6291456 | tf_op jit(solution)/shard_map/attend/pallas_call | solution.py:198
  66.1 2.1 %collective-permute-start.1 = (bf16[8,160,128]{2,1,0:T(8,128)(2,1)S(1)}, bf16[8,160,128]{2,1,0:T(8,128)(2,1)S(1)}, u32[]{:S(2)}, u32[]{:S(2)}) collective-permute-start(bf16[8,160,128]{2,1,0:T(8,128)(2,1)S(1)} %attend.7), channel_id=1, source_target_pairs={{0,32},{32,0},{1,33},{33,1},{2,34},{34,2},{3,35},{35,3},{4,36},{36... | collective-permute-start | bytes 983048 | tf_op jit(solution)/shard_map/ppermute | solution.py:305
  68.2 0.0 copy-done.4
  68.2 6.4 %attend.6.own_ref = bf16[8,160,128]{2,1,0:T(8,128)(2,1)S(1)} custom-call(s32[1]{0:T(128)} %bitcast.3.side_ref, bf16[8,2,144,128]{3,2,1,0:T(8,128)(2,1)S(1)} %bitcast.12, bf16[32,256,128]{2,1,0:T(8,128)(2,1)S(1)} %all-to-all-done.5.kv_ref), custom_call_target="tpu_custom_call" | custom-call | flops 4831838208 | bytes 6291456 | tf_op jit(solution)/shard_map/attend/pallas_call | solution.py:198
  74.6 0.0 copy-start.5
  74.6 0.0 copy-start.7
  74.6 0.0 collective-permute-done.1.other_ref
  74.6 1.6 %merge_pair.3 = bf16[8,160,128]{2,1,0:T(8,128)(2,1)} custom-call(bf16[8,160,128]{2,1,0:T(8,128)(2,1)S(1)} %attend.6.own_ref, bf16[8,160,128]{2,1,0:T(8,128)(2,1)S(1)} %collective-permute-done.1.other_ref), custom_call_target="tpu_custom_call" | custom-call | tf_op jit(solution)/shard_map/merge_pair/pallas_call | solution.py:231
  76.2 8.6 %all-to-all-start.6 = ((bf16[8,160,128]{2,1,0:T(8,128)(2,1)}), bf16[8,160,128]{2,1,0:T(8,128)(2,1)S(1)}, u32[]{:S(2)}, u32[]{:S(2)}) async-start(bf16[8,160,128]{2,1,0:T(8,128)(2,1)} %merge_pair.3), calls=%async_computation.6 | async-start | bytes 655360 | tf_op jit(solution)/shard_map/all_to_all | solution.py:293
  85.4 0.0 copy-done
  85.5 15.5 %all-to-all-done.6.parts_ref = bf16[8,160,128]{2,1,0:T(8,128)(2,1)S(1)} async-done(((bf16[8,160,128]{2,1,0:T(8,128)(2,1)}), bf16[8,160,128]{2,1,0:T(8,128)(2,1)S(1)}, u32[]{:S(2)}, u32[]{:S(2)}) %all-to-all-start.6) | async-done | bytes 327712 | tf_op jit(solution)/shard_map/all_to_all | solution.py:293
  100.9 1.2 finish.3
  102.2 15.0 %all-to-all-start.7 = ((bf16[32,8,128]{2,1,0:T(8,128)(2,1)}), bf16[32,8,128]{2,1,0:T(8,128)(2,1)S(1)}, u32[]{:S(2)}, u32[]{:S(2)}) async-start(bf16[32,8,128]{2,1,0:T(8,128)(2,1)} %finish.3), calls=%async_computation.7 | async-start | bytes 131072 | tf_op jit(solution)/shard_map/all_to_all | solution.py:293
  117.2 1.4 %fusion = f32[]{:T(128)} fusion(bf16[8,2,144,128]{3,2,1,0:T(8,128)(2,1)} %bitcast.10), kind=kLoop, calls=%fused_computation.1 | loop fusion | flops 31 | bytes 36 | tf_op jit(solution)/shard_map/reduce_min | solution.py:316
  119.3 5.1 %all-to-all-done.7.rows_ref = bf16[32,8,128]{2,1,0:T(8,128)(2,1)S(1)} async-done(((bf16[32,8,128]{2,1,0:T(8,128)(2,1)}), bf16[32,8,128]{2,1,0:T(8,128)(2,1)S(1)}, u32[]{:S(2)}, u32[]{:S(2)}) %all-to-all-start.7) | async-done | bytes 65568 | tf_op jit(solution)/shard_map/all_to_all | solution.py:293
  124.4 0.0 copy-done.5
  124.4 0.0 copy-done.7
  124.4 0.3 conditional.1
  124.7 0.0 copy-start.6
  124.7 0.6 copy-done.6
  (2 shorter events, 0.0 us)
Async XLA Ops:
  0.0 85.4 %copy-start = (f32[50,4096]{1,0:T(8,128)S(1)}, f32[50,4096]{1,0:T(8,128)}, u32[]{:S(2)}) copy-start(f32[50,4096]{1,0:T(8,128)} %param.15) | copy-start | bytes 2457604
  2.9 17.6 %all-to-all-start.4 = ((bf16[32,8,128]{2,1,0:T(8,128)(2,1)}), bf16[32,8,128]{2,1,0:T(8,128)(2,1)S(1)}, u32[]{:S(2)}, u32[]{:S(2)}) async-start(bf16[32,8,128]{2,1,0:T(8,128)(2,1)} %choose.3), calls=%async_computation.4 | async-start | bytes 131072 | tf_op jit(solution)/shard_map/all_to_all | solution.py:293
  20.5 38.0 %all-to-all-start.5 = ((bf16[32,256,128]{2,1,0:T(8,128)(2,1)}), bf16[32,256,128]{2,1,0:T(8,128)(2,1)S(1)}, u32[]{:S(2)}, u32[]{:S(2)}) async-start(bf16[32,256,128]{2,1,0:T(8,128)(2,1)} %split_heads.3), calls=%async_computation.5 | async-start | bytes 4194304 | tf_op jit(solution)/shard_map/all_to_all | solution.py:293
  58.5 1.1 copy-start.3
  59.6 8.6 %copy-start.4 = (bf16[2304,128]{1,0:T(8,128)(2,1)S(1)}, bf16[2304,128]{1,0:T(8,128)(2,1)}, u32[]{:S(2)}) copy-start(bf16[2304,128]{1,0:T(8,128)(2,1)} %all-gather.1) | copy-start | bytes 1769476
  66.1 8.6 %collective-permute-start.1 = (bf16[8,160,128]{2,1,0:T(8,128)(2,1)S(1)}, bf16[8,160,128]{2,1,0:T(8,128)(2,1)S(1)}, u32[]{:S(2)}, u32[]{:S(2)}) collective-permute-start(bf16[8,160,128]{2,1,0:T(8,128)(2,1)S(1)} %attend.7), channel_id=1, source_target_pairs={{0,32},{32,0},{1,33},{33,1},{2,34},{34,2},{3,35},{35,3},{4,36},{36... | collective-permute-start | bytes 983048 | tf_op jit(solution)/shard_map/ppermute | solution.py:305
  74.6 49.8 %copy-start.5 = (bf16[128,4096]{1,0:T(8,128)(2,1)S(1)}, bf16[128,4096]{1,0:T(8,128)(2,1)}, u32[]{:S(2)}) copy-start(bf16[128,4096]{1,0:T(8,128)(2,1)} %query_ref.1) | copy-start | bytes 3145732
  74.6 49.8 %copy-start.7 = (s32[6]{0:T(128)S(1)}, s32[6]{0:T(128)}, u32[]{:S(2)}) copy-start(s32[6]{0:T(128)} %index_ref.1) | copy-start | bytes 76
  76.2 24.7 %all-to-all-start.6 = ((bf16[8,160,128]{2,1,0:T(8,128)(2,1)}), bf16[8,160,128]{2,1,0:T(8,128)(2,1)S(1)}, u32[]{:S(2)}, u32[]{:S(2)}) async-start(bf16[8,160,128]{2,1,0:T(8,128)(2,1)} %merge_pair.3), calls=%async_computation.6 | async-start | bytes 655360 | tf_op jit(solution)/shard_map/all_to_all | solution.py:293
  102.2 22.2 %all-to-all-start.7 = ((bf16[32,8,128]{2,1,0:T(8,128)(2,1)}), bf16[32,8,128]{2,1,0:T(8,128)(2,1)S(1)}, u32[]{:S(2)}, u32[]{:S(2)}) async-start(bf16[32,8,128]{2,1,0:T(8,128)(2,1)} %finish.3), calls=%async_computation.7 | async-start | bytes 131072 | tf_op jit(solution)/shard_map/all_to_all | solution.py:293
  124.7 0.6 copy-start.6

commit v5 on v4

--- a/solution.py
+++ b/solution.py
@@ -225,15 +225,11 @@
 
 
 def merge_pair(own, other):
-    group = 4
-    msg = own.shape[1]
-    spec = pl.BlockSpec((group, msg, HD), lambda i: (i, 0, 0))
-    return pl.pallas_call(
-        functools.partial(pair_body, group, msg - TAIL),
-        grid=(NZO // group,),
-        in_specs=[spec, spec],
-        out_specs=spec,
-        out_shape=jax.ShapeDtypeStruct((NZO, msg, HD), BF),
+    return pl.pallas_call(
+        functools.partial(pair_body, NZO, own.shape[1] - TAIL),
+        out_shape=jax.ShapeDtypeStruct(own.shape, BF),
+        in_specs=[VMEM, VMEM],
+        out_specs=VMEM,
         compiler_params=SMALL,
         name="merge_pair",
     )(own, other)
@@ -293,7 +289,7 @@
     return lax.all_to_all(x, axes, split_axis=0, concat_axis=0, tiled=True)
 
 
-def whole(kept, query, key, value, index, counts, gate):
+def whole(kept, query, key, value, index, counts):
     side = lax.axis_index("zi").astype(jnp.int32).reshape(1)
     mine = choose(query, index, counts)
     kv = split_heads(key, value)
@@ -306,13 +302,12 @@
     own = attend(side, rows, kv)
     merged = merge_pair(own, arrived)
     parts = swap(merged, "zo")
-    heads = swap(finish(parts, live, back), PLANE)
-    return apply_gate(counts, heads, gate), rows
+    return swap(finish(parts, live, back), PLANE), rows
 
 
 def local(query, key, value, index, counts, timestep, gate_table):
     gate = lax.dynamic_slice_in_dim(gate_table, timestep[0], 1, 0)
-    usual, rows = whole(FIRST, query, key, value, index, counts, gate)
+    usual, rows = whole(FIRST, query, key, value, index, counts)
     full = jnp.min(rows[:, :, FIRST - 1, 0].astype(F32)) < DEAD / 2
     full, usual = lax.optimization_barrier((full, usual))
 
@@ -322,7 +317,8 @@
     def keep(usual, *args):
         return usual
 
-    return lax.cond(full, again, keep, usual, query, key, value, index, counts, gate)
+    heads = lax.cond(full, again, keep, usual, query, key, value, index, counts)
+    return apply_gate(counts, heads, gate)
 
 
 def solution(mesh):

time: 126 us -> 126 us (level)
  no operation moved by 1% of the time
where the time goes in v5:
time: 126 us; the launch traced here: 125 us
  starting transfers between devices  40.5 us (32%)
  blocking collectives  33.1 us (26%)
  waiting for transfers between devices  23.7 us (19%)
  Pallas kernels  22.9 us (18%)
  between operations  2.14 us (2%)
  other arithmetic  1.42 us (1%)
    all_to_all x4, starting transfers between devices, swap(): return lax.all_to_all(x, axes, split_axis=0, concat_axis=0, tiled=True)  38.4 us
    all_gather x1, blocking collectives, whole(): lax.all_gather(live, ('zo', 'zi'), axis=0, tiled=False)  33.1 us
    all_to_all x4, waiting for transfers between devices, swap(): return lax.all_to_all(x, axes, split_axis=0, concat_axis=0, tiled=True)  23.7 us
    pallas_call x2, Pallas kernels, attend(): pl.pallas_call(attend_body, out_shape=jax.ShapeDtypeStruct((NZO, rows + T...  12.9 us
    pallas_call x1, Pallas kernels, split_heads(): pl.pallas_call(functools.partial(split_body, per), grid=(HEADS // per,),...  3.92 us
  transfers between devices with their start and end apart: 5, of which 3 were waited for; matrix products, arithmetic and copies ran while one was open for 1% of the time, Pallas kernels for 9%

profile of v5, /device:TPU:1, one launch (start us, length us, event | category | flops | bytes accessed | tf_op | source)
XLA Modules:
  0.0 124.9 jit_solution(2563894620638339831)
XLA Ops:
  0.0 0.0 copy-start
  0.7 2.1 %choose.3 = bf16[32,8,128]{2,1,0:T(8,128)(2,1)} custom-call(s32[6]{0:T(128)} %index_ref.1, s32[1]{0:T(128)S(6)} %copy.10.count_ref, bf16[128,4096]{1,0:T(8,128)(2,1)} %query_ref.1), custom_call_target="tpu_custom_call" | custom-call | tf_op jit(solution)/shard_map/choose/pallas_call | solution.py:53
  2.9 10.5 %all-to-all-start.4 = ((bf16[32,8,128]{2,1,0:T(8,128)(2,1)}), bf16[32,8,128]{2,1,0:T(8,128)(2,1)S(1)}, u32[]{:S(2)}, u32[]{:S(2)}) async-start(bf16[32,8,128]{2,1,0:T(8,128)(2,1)} %choose.3), calls=%async_computation.4 | async-start | bytes 131072 | tf_op jit(solution)/shard_map/all_to_all | solution.py:289
  13.4 3.9 %split_heads.3 = bf16[32,256,128]{2,1,0:T(8,128)(2,1)} custom-call(bf16[128,4096]{1,0:T(8,128)(2,1)} %key_ref.1, bf16[128,4096]{1,0:T(8,128)(2,1)} %value_ref.1), custom_call_target="tpu_custom_call" | custom-call | tf_op jit(solution)/shard_map/split_heads/pallas_call | solution.py:70
  17.3 3.2 %all-to-all-done.4.rows_ref = bf16[32,8,128]{2,1,0:T(8,128)(2,1)S(1)} async-done(((bf16[32,8,128]{2,1,0:T(8,128)(2,1)}), bf16[32,8,128]{2,1,0:T(8,128)(2,1)S(1)}, u32[]{:S(2)}, u32[]{:S(2)}) %all-to-all-start.4) | async-done | bytes 65568 | tf_op jit(solution)/shard_map/all_to_all | solution.py:289
  20.5 4.3 %all-to-all-start.5 = ((bf16[32,256,128]{2,1,0:T(8,128)(2,1)}), bf16[32,256,128]{2,1,0:T(8,128)(2,1)S(1)}, u32[]{:S(2)}, u32[]{:S(2)}) async-start(bf16[32,256,128]{2,1,0:T(8,128)(2,1)} %split_heads.3), calls=%async_computation.5 | async-start | bytes 4194304 | tf_op jit(solution)/shard_map/all_to_all | solution.py:289
  24.8 0.6 compact.3
  25.4 33.1 %all-gather.1 = bf16[2304,128]{1,0:T(8,128)(2,1)} all-gather(bf16[144,128]{1,0:T(8,128)(2,1)S(1)} %get-tuple-element.32.live_ref), channel_id=3, replica_groups=mesh['zo'=8,'zi'=2,'c'=2,'blk'=16] {'zo','zi'}, dimensions={0}, use_global_device_ids=true | all-gather | bytes 626688 | tf_op jit(solution)/shard_map/all_gather | solution.py:299
  58.5 0.0 all-to-all-done.5.kv_ref
  58.5 0.0 copy-start.3
  58.5 1.1 copy-done.3
  59.6 0.0 copy-start.4
  59.6 6.5 %attend.7 = bf16[8,160,128]{2,1,0:T(8,128)(2,1)S(1)} custom-call(s32[1]{0:T(128)S(6)} %sub.6.side_ref, bf16[8,2,144,128]{3,2,1,0:T(8,128)(2,1)S(1)} %bitcast.11, bf16[32,256,128]{2,1,0:T(8,128)(2,1)S(1)} %all-to-all-done.5.kv_ref), custom_call_target="tpu_custom_call" | custom-call | flops 4831838208 | bytes 6291456 | tf_op jit(solution)/shard_map/attend/pallas_call | solution.py:198
  66.1 2.1 %collective-permute-start.1 = (bf16[8,160,128]{2,1,0:T(8,128)(2,1)S(1)}, bf16[8,160,128]{2,1,0:T(8,128)(2,1)S(1)}, u32[]{:S(2)}, u32[]{:S(2)}) collective-permute-start(bf16[8,160,128]{2,1,0:T(8,128)(2,1)S(1)} %attend.7), channel_id=1, source_target_pairs={{0,32},{32,0},{1,33},{33,1},{2,34},{34,2},{3,35},{35,3},{4,36},{36... | collective-permute-start | bytes 983048 | tf_op jit(solution)/shard_map/ppermute | solution.py:301
  68.2 0.0 copy-done.4
  68.2 6.4 %attend.6.own_ref = bf16[8,160,128]{2,1,0:T(8,128)(2,1)S(1)} custom-call(s32[1]{0:T(128)} %bitcast.3.side_ref, bf16[8,2,144,128]{3,2,1,0:T(8,128)(2,1)S(1)} %bitcast.12, bf16[32,256,128]{2,1,0:T(8,128)(2,1)S(1)} %all-to-all-done.5.kv_ref), custom_call_target="tpu_custom_call" | custom-call | flops 4831838208 | bytes 6291456 | tf_op jit(solution)/shard_map/attend/pallas_call | solution.py:198
  74.6 0.0 copy-start.5
  74.6 0.0 copy-start.6
  74.6 0.0 collective-permute-done.1.other_ref
  74.6 1.5 %merge_pair.3 = bf16[8,160,128]{2,1,0:T(8,128)(2,1)} custom-call(bf16[8,160,128]{2,1,0:T(8,128)(2,1)S(1)} %attend.6.own_ref, bf16[8,160,128]{2,1,0:T(8,128)(2,1)S(1)} %collective-permute-done.1.other_ref), custom_call_target="tpu_custom_call" | custom-call | tf_op jit(solution)/shard_map/merge_pair/pallas_call | solution.py:228
  76.1 8.6 %all-to-all-start.6 = ((bf16[8,160,128]{2,1,0:T(8,128)(2,1)}), bf16[8,160,128]{2,1,0:T(8,128)(2,1)S(1)}, u32[]{:S(2)}, u32[]{:S(2)}) async-start(bf16[8,160,128]{2,1,0:T(8,128)(2,1)} %merge_pair.3), calls=%async_computation.6 | async-start | bytes 655360 | tf_op jit(solution)/shard_map/all_to_all | solution.py:289
  85.3 0.0 copy-done
  85.4 15.5 %all-to-all-done.6.parts_ref = bf16[8,160,128]{2,1,0:T(8,128)(2,1)S(1)} async-done(((bf16[8,160,128]{2,1,0:T(8,128)(2,1)}), bf16[8,160,128]{2,1,0:T(8,128)(2,1)S(1)}, u32[]{:S(2)}, u32[]{:S(2)}) %all-to-all-start.6) | async-done | bytes 327712 | tf_op jit(solution)/shard_map/all_to_all | solution.py:289
  100.8 1.2 finish.3
  102.1 15.0 %all-to-all-start.7 = ((bf16[32,8,128]{2,1,0:T(8,128)(2,1)}), bf16[32,8,128]{2,1,0:T(8,128)(2,1)S(1)}, u32[]{:S(2)}, u32[]{:S(2)}) async-start(bf16[32,8,128]{2,1,0:T(8,128)(2,1)} %finish.3), calls=%async_computation.7 | async-start | bytes 131072 | tf_op jit(solution)/shard_map/all_to_all | solution.py:289
  117.1 1.4 %fusion = f32[]{:T(128)} fusion(bf16[8,2,144,128]{3,2,1,0:T(8,128)(2,1)} %bitcast.10), kind=kLoop, calls=%fused_computation.1 | loop fusion | flops 31 | bytes 36 | tf_op jit(solution)/shard_map/reduce_min | solution.py:311
  119.2 5.1 %all-to-all-done.7 = bf16[32,8,128]{2,1,0:T(8,128)(2,1)S(1)} async-done(((bf16[32,8,128]{2,1,0:T(8,128)(2,1)}), bf16[32,8,128]{2,1,0:T(8,128)(2,1)S(1)}, u32[]{:S(2)}, u32[]{:S(2)}) %all-to-all-start.7) | async-done | bytes 65568 | tf_op jit(solution)/shard_map/all_to_all | solution.py:289
  124.3 0.0 copy-done.5
  124.3 0.0 copy-done.6
  124.3 0.7 apply_gate.1
  (2 shorter events, 0.0 us)
Async XLA Ops:
  0.0 85.3 %copy-start = (f32[50,4096]{1,0:T(8,128)S(1)}, f32[50,4096]{1,0:T(8,128)}, u32[]{:S(2)}) copy-start(f32[50,4096]{1,0:T(8,128)} %param.15) | copy-start | bytes 2457604
  2.9 17.6 %all-to-all-start.4 = ((bf16[32,8,128]{2,1,0:T(8,128)(2,1)}), bf16[32,8,128]{2,1,0:T(8,128)(2,1)S(1)}, u32[]{:S(2)}, u32[]{:S(2)}) async-start(bf16[32,8,128]{2,1,0:T(8,128)(2,1)} %choose.3), calls=%async_computation.4 | async-start | bytes 131072 | tf_op jit(solution)/shard_map/all_to_all | solution.py:289
  20.5 38.0 %all-to-all-start.5 = ((bf16[32,256,128]{2,1,0:T(8,128)(2,1)}), bf16[32,256,128]{2,1,0:T(8,128)(2,1)S(1)}, u32[]{:S(2)}, u32[]{:S(2)}) async-start(bf16[32,256,128]{2,1,0:T(8,128)(2,1)} %split_heads.3), calls=%async_computation.5 | async-start | bytes 4194304 | tf_op jit(solution)/shard_map/all_to_all | solution.py:289
  58.5 1.1 copy-start.3
  59.6 8.6 %copy-start.4 = (bf16[2304,128]{1,0:T(8,128)(2,1)S(1)}, bf16[2304,128]{1,0:T(8,128)(2,1)}, u32[]{:S(2)}) copy-start(bf16[2304,128]{1,0:T(8,128)(2,1)} %all-gather.1) | copy-start | bytes 1769476
  66.1 8.6 %collective-permute-start.1 = (bf16[8,160,128]{2,1,0:T(8,128)(2,1)S(1)}, bf16[8,160,128]{2,1,0:T(8,128)(2,1)S(1)}, u32[]{:S(2)}, u32[]{:S(2)}) collective-permute-start(bf16[8,160,128]{2,1,0:T(8,128)(2,1)S(1)} %attend.7), channel_id=1, source_target_pairs={{0,32},{32,0},{1,33},{33,1},{2,34},{34,2},{3,35},{35,3},{4,36},{36... | collective-permute-start | bytes 983048 | tf_op jit(solution)/shard_map/ppermute | solution.py:301
  74.6 49.7 %copy-start.5 = (bf16[128,4096]{1,0:T(8,128)(2,1)S(1)}, bf16[128,4096]{1,0:T(8,128)(2,1)}, u32[]{:S(2)}) copy-start(bf16[128,4096]{1,0:T(8,128)(2,1)} %query_ref.1) | copy-start | bytes 3145732
  74.6 49.7 %copy-start.6 = (s32[6]{0:T(128)S(1)}, s32[6]{0:T(128)}, u32[]{:S(2)}) copy-start(s32[6]{0:T(128)} %index_ref.1) | copy-start | bytes 76
  76.1 24.7 %all-to-all-start.6 = ((bf16[8,160,128]{2,1,0:T(8,128)(2,1)}), bf16[8,160,128]{2,1,0:T(8,128)(2,1)S(1)}, u32[]{:S(2)}, u32[]{:S(2)}) async-start(bf16[8,160,128]{2,1,0:T(8,128)(2,1)} %merge_pair.3), calls=%async_computation.6 | async-start | bytes 655360 | tf_op jit(solution)/shard_map/all_to_all | solution.py:289
  102.1 22.2 %all-to-all-start.7 = ((bf16[32,8,128]{2,1,0:T(8,128)(2,1)}), bf16[32,8,128]{2,1,0:T(8,128)(2,1)S(1)}, u32[]{:S(2)}, u32[]{:S(2)}) async-start(bf16[32,8,128]{2,1,0:T(8,128)(2,1)} %finish.3), calls=%async_computation.7 | async-start | bytes 131072 | tf_op jit(solution)/shard_map/all_to_all | solution.py:289
